TPU v7x, 256 devices: a whole 4x4x8 slice. The times are simulated.
256 devices in a mesh: section: 2 (over z_lo), tok: 16 (over x, y), wid: 8 (over z_hi, core).
Axes of the slice: x: 4, y: 4, z: 8 (z_hi: 4, z_lo: 2; z = z_hi * 2 + z_lo), core: 2. Of those that a mesh axis runs over, the one named last changes fastest.
Arguments:
- hidden: bfloat16 [4096, 24576], P('wid', ('section', 'tok')), may hold values from -6 to 6
- resid: bfloat16 [4096, 12288], P('wid', ('section', 'tok')), may hold values from -8 to 8
- down_weight: bfloat16 [24576, 12288], P(('section', 'tok'), 'wid'), may hold values from -0.078125 to 0.078125
- down_bias: float32 [12288], P(('section', 'tok')), may hold values from -3 to 3
- norm_gain: float32 [12288], P('wid'), may hold values from 0.1 to 1.9
- norm_shift: float32 [12288], P('wid'), may hold values from -3 to 3
- query_weight: bfloat16 [12288, 12288], P('wid', ('section', 'tok')), may hold values from -0.109375 to 0.109375
- query_bias: float32 [12288], P('wid'), may hold values from -3 to 3
Outputs:
- stream: bfloat16 [4096, 12288], P('wid', ('section', 'tok'))
- query: bfloat16 [8, 512, 12288], P(None, ('section', 'tok'), 'wid')
All inputs are finite; a program needn't handle non-finite values.
Results may differ from a plain program's by a relative error of at most 0.029.
Values may be sent and summed in bfloat16 or wider, within the bound.
A program may use at most 128 MiB of HBM per device.

v0:
```python
import jax
import jax.numpy as jnp
from jax import lax
from jax.sharding import PartitionSpec as P

norm_eps = 1e-05


def per_device(
    hidden, resid, down_weight, down_bias, norm_gain, norm_shift, query_weight, query_bias
):
    down_terms = jnp.dot(
        hidden,
        lax.all_gather(down_weight, "wid", axis=1, tiled=True),
        preferred_element_type=jnp.float32,
    )
    down_share = lax.psum_scatter(
        down_terms.astype(jnp.bfloat16), ("section", "tok"), scatter_dimension=1, tiled=True
    ).astype(jnp.float32)
    stream = (resid.astype(jnp.float32) + down_share + down_bias).astype(jnp.bfloat16)
    wid_count = lax.axis_size("wid")
    wid_index = lax.axis_index("wid")
    feature_width = norm_gain.shape[0]
    regrouped = lax.all_to_all(stream, ("section", "tok"), split_axis=0, concat_axis=1, tiled=True)
    token_rows = lax.all_gather(regrouped, "wid", axis=0, tiled=True)
    row_values = token_rows.astype(jnp.float32)
    row_mean = jnp.mean(row_values, axis=-1, keepdims=True)
    centred = row_values - row_mean
    row_var = jnp.mean(centred * centred, axis=-1, keepdims=True)
    own_cols = lax.dynamic_slice_in_dim(centred, wid_index * feature_width, feature_width, 1)
    normed = (own_cols * lax.rsqrt(row_var + norm_eps) * norm_gain + norm_shift).astype(
        jnp.bfloat16
    )
    query_terms = jnp.dot(
        normed,
        lax.all_gather(query_weight, ("section", "tok"), axis=1, tiled=True),
        preferred_element_type=jnp.float32,
    )
    query_share = lax.psum_scatter(
        query_terms.astype(jnp.bfloat16), "wid", scatter_dimension=1, tiled=True
    ).astype(jnp.float32)
    query = (query_share + query_bias).astype(jnp.bfloat16)
    query = query.reshape(wid_count, query.shape[0] // wid_count, query.shape[1])
    return (stream, query)


def solution(mesh):
    return jax.shard_map(
        per_device,
        mesh=mesh,
        in_specs=(
            P("wid", ("section", "tok")),
            P("wid", ("section", "tok")),
            P(("section", "tok"), "wid"),
            P(("section", "tok")),
            P("wid"),
            P("wid"),
            P("wid", ("section", "tok")),
            P("wid"),
        ),
        out_specs=(P("wid", ("section", "tok")), P(None, ("section", "tok"), "wid")),
        check_vma=False,
    )
```

profile of v0, /device:TPU:12, one launch (start us, length us, event | category | flops | bytes accessed | tf_op | source)
XLA Modules:
  0.0 956.4 jit_solution(10747772127501058328)
XLA Ops:
  7.2 0.0 all-gather.4.cloned.1.call-start
  7.2 0.7 all-gather.4.cloned.1.call-update
  7.9 0.0 reduce-scatter.7.cloned.1.call-start
  8.0 178.1 %all-gather.4.cloned.1.call-done = bf16[768,12288]{1,0:T(8,128)(2,1)} async-done(((bf16[768,1536]{1,0:T(8,128)(2,1)}), bf16[768,12288]{1,0:T(8,128)(2,1)}) %all-gather.4.cloned.1.call-update) | async-done | bytes 18874384 | tf_op jit(solution)/shard_map/all_gather | solution.py:14
  186.1 18.6 %convolution_convert_fusion = bf16[512,12288]{1,0:T(8,128)(2,1)} fusion(bf16[512,768]{1,0:T(8,128)(2,1)S(1)} %copy-done, bf16[768,12288]{1,0:T(8,128)(2,1)} %all-gather.4.cloned.1.call-done), kind=kOutput, calls=%fused_computation | convolution fusion | flops 9669967872 | bytes 32243712 | tf_op jit(solution)/shard_map/dot_general | solution.py:12
  204.7 16.7 %copy.12 = bf16[512,12288]{0,1:T(8,128)(2,1)} copy(bf16[512,12288]{1,0:T(8,128)(2,1)} %convolution_convert_fusion) | data formatting | bytes 25165824
  221.4 0.0 reduce-scatter.7.cloned.1.call-update
  221.4 0.0 all-gather.6.cloned.1.call-start
  221.5 178.1 %reduce-scatter.7.cloned.1.call-done = bf16[384,512]{1,0:T(8,128)(2,1)} async-done(((bf16[12288,512]{1,0:T(8,128)(2,1)}), bf16[384,512]{1,0:T(8,128)(2,1)}) %reduce-scatter.7.cloned.1.call-update) | async-done | bytes 393232
  399.5 1.2 copy.13
  400.8 0.1 add_convert_fusion.2
  400.9 25.0 %all_to_all.19 = bf16[32,16,384]{2,1,0:T(8,128)(2,1)S(1)} all-to-all(bf16[32,16,384]{2,1,0:T(8,128)(2,1)S(1)} %bitcast.13), channel_id=1, replica_groups=mesh['section'=2,'tok'=16,'wid'=8] {'section','tok'}, dimensions={0} | all-to-all | bytes 786432 | tf_op jit(solution)/shard_map/all_to_all | solution.py:24
  425.9 0.8 copy.14
  426.8 0.0 all-gather.8.cloned.1.call-start
  426.8 0.5 all-gather.8.cloned.1.call-update
  427.3 0.0 reduce-scatter.5.cloned.1.call-start
  427.4 44.9 %all-gather.6.cloned.1.call-done = bf16[128,12288]{1,0:T(8,128)(2,1)} async-done(((bf16[16,12288]{1,0:T(8,128)(2,1)}), bf16[128,12288]{1,0:T(8,128)(2,1)}) %all-gather.6.cloned.1.call-update) | async-done | bytes 3145744 | tf_op jit(solution)/shard_map/all_gather | solution.py:25
  472.3 2.4 convert_reduce_fusion
  474.7 5.4 multiply_reduce_fusion
  480.1 398.5 %all-gather.8.cloned.1.call-done = bf16[1536,12288]{1,0:T(8,128)(2,1)} async-done(((bf16[1536,384]{1,0:T(8,128)(2,1)}), bf16[1536,12288]{1,0:T(8,128)(2,1)}) %all-gather.8.cloned.1.call-update) | async-done | bytes 37748752 | tf_op jit(solution)/shard_map/all_gather | solution.py:36
  878.6 16.5 %convolution_convert_fusion.1 = bf16[128,12288]{1,0:T(8,128)(2,1)} fusion(bf16[1536,12288]{1,0:T(8,128)(2,1)} %all-gather.8.cloned.1.call-done, f32[128,12288]{1,0:T(8,128)} %get-tuple-element.3, s32[]{:T(128)S(6)} %select_n.3, f32[1536]{0:T(1024)S(1)} %copy-done.4, f32[1536]{0:T(1024)S(1)} %copy-done.5, f32[128]{0:T(128)S(1)} %add_rsqrt_fusion), kind=kOutput, calls=%fused_computation.1 | convolution fusion | flops 4834197504 | bytes 41693700 | tf_op jit(solution)/shard_map/dot_general | solution.py:34
  895.2 0.0 reduce-scatter.5.cloned.1.call-update
  895.2 52.9 %reduce-scatter.5.cloned.1.call-done = bf16[128,1536]{1,0:T(8,128)(2,1)} async-done(((bf16[128,12288]{1,0:T(8,128)(2,1)}), bf16[128,1536]{1,0:T(8,128)(2,1)}) %reduce-scatter.5.cloned.1.call-update) | async-done | bytes 393232 | tf_op jit(solution)/shard_map/reduce_scatter | solution.py:39
  948.1 1.8 add_convert_fusion
  (19 shorter events, 0.1 us)
Async XLA Ops:
  7.2 178.9 %copy-start = (bf16[512,768]{1,0:T(8,128)(2,1)S(1)}, bf16[512,768]{1,0:T(8,128)(2,1)}, u32[]{:S(2)}) copy-start(bf16[512,768]{1,0:T(8,128)(2,1)} %param.8) | copy-start | bytes 2359300
  7.2 178.9 %all-gather.4.cloned.1.call-start = ((), (), s32[]{:S(2)}) async-start(), calls=%async_computation.3 | async-start | bytes 21233664 | tf_op jit(solution)/shard_map/all_gather | solution.py:14
  7.9 391.6 %reduce-scatter.7.cloned.1.call-start = ((), (), s32[]{:S(2)}) async-start(), calls=%async_computation.7 | async-start | bytes 12976128
  221.4 179.4 %copy-start.3 = (bf16[512,384]{1,0:T(8,128)(2,1)S(1)}, bf16[512,384]{1,0:T(8,128)(2,1)}, u32[]{:S(2)}) copy-start(bf16[512,384]{1,0:T(8,128)(2,1)} %param.9) | copy-start | bytes 1179652
  221.4 179.4 %copy-start.7 = (f32[384]{0:T(512)S(1)}, f32[384]{0:T(512)}, u32[]{:S(2)}) copy-start(f32[384]{0:T(512)} %param.11) | copy-start | bytes 4612
  221.4 250.9 %all-gather.6.cloned.1.call-start = ((), (), s32[]{:S(2)}) async-start(), calls=%async_computation.4 | async-start | bytes 3538944 | tf_op jit(solution)/shard_map/all_gather | solution.py:25
  400.9 79.2 %copy-start.2 = (bf16[512,384]{1,0:T(8,128)(2,1)}, bf16[512,384]{1,0:T(8,128)(2,1)S(1)}, u32[]{:S(2)}) copy-start(bf16[512,384]{1,0:T(8,128)(2,1)S(1)} %add_convert_fusion.2) | copy-start | bytes 1179652
  426.8 451.9 %all-gather.8.cloned.1.call-start = ((), (), s32[]{:S(2)}) async-start(), calls=%async_computation.5 | async-start | bytes 38928384 | tf_op jit(solution)/shard_map/all_gather | solution.py:36
  427.3 520.8 %reduce-scatter.5.cloned.1.call-start = ((), (), s32[]{:S(2)}) async-start(), calls=%async_computation.6 | async-start | bytes 3538944 | tf_op jit(solution)/shard_map/reduce_scatter | solution.py:39
  427.4 451.3 %copy-start.4 = (f32[1536]{0:T(1024)S(1)}, f32[1536]{0:T(1024)}, u32[]{:S(2)}) copy-start(f32[1536]{0:T(1024)} %param.13) | copy-start | bytes 18436
  427.4 451.2 %copy-start.5 = (f32[1536]{0:T(1024)S(1)}, f32[1536]{0:T(1024)}, u32[]{:S(2)}) copy-start(f32[1536]{0:T(1024)} %param.12) | copy-start | bytes 18436
  878.6 69.5 %copy-start.6 = (f32[1536]{0:T(1024)S(1)}, f32[1536]{0:T(1024)}, u32[]{:S(2)}) copy-start(f32[1536]{0:T(1024)} %param.15) | copy-start | bytes 18436
  878.6 71.3 %copy-start.1 = (bf16[512,768]{1,0:T(8,128)(2,1)S(1)}, bf16[512,768]{1,0:T(8,128)(2,1)}, u32[]{:S(2)}) copy-start(bf16[512,768]{1,0:T(8,128)(2,1)} %param.8) | copy-start | bytes 2359300
Sparse Core Ops, SparseCore 0:
  9.9 176.2 all-gather.3
  221.5 177.9 reduce-scatter.6
  426.9 45.3 all-gather.5
  473.9 404.6 all-gather.7
  895.3 52.7 reduce-scatter.4
where the time goes:
time: 957 us; the launch traced here: 956 us
  waiting for transfers between devices  854 us (89%)
  matrix products  35.2 us (4%)
  blocking collectives  25 us (3%)
  local copies, waits for them, and re-layouts  18.7 us (2%)
  between operations  13.9 us (1%)
  other arithmetic  9.72 us (1%)
    all_gather x1, waiting for transfers between devices, per_device(): lax.all_gather(query_weight, ('section', 'tok'), axis=1, tiled=True)  399 us
    unnamed x6, waiting for transfers between devices  179 us
    all_gather x1, waiting for transfers between devices, per_device(): lax.all_gather(down_weight, 'wid', axis=1, tiled=True)  178 us
    reduce_scatter x1, waiting for transfers between devices, per_device(): lax.psum_scatter(query_terms.astype(jnp.bfloat16), 'wid', scatter_dimensi...  52.9 us
    all_gather x1, waiting for transfers between devices, per_device(): token_rows = lax.all_gather(regrouped, 'wid', axis=0, tiled=True)  44.9 us
    all_to_all x1, blocking collectives, per_device(): lax.all_to_all(stream, ('section', 'tok'), split_axis=0, concat_axis=1, t...  25 us
  transfers between devices with their start and end apart: 5, of which 5 were waited for; matrix products, arithmetic and copies ran while one was open for 1% of the time, Pallas kernels for 0%

commit v1 on v0

v1 whole, which is shorter than its diff:
```python
import jax
import jax.numpy as jnp
from jax import lax
from jax.sharding import PartitionSpec as P

norm_eps = 1e-05
ST = ("section", "tok")


def per_device(
    hidden, resid, down_weight, down_bias, norm_gain, norm_shift, query_weight, query_bias
):
    wid_count = lax.axis_size("wid")
    st_count = lax.axis_size("section") * lax.axis_size("tok")
    wid_index = lax.axis_index("wid")
    width = norm_gain.shape[0]
    rows = resid.shape[0] // st_count
    resid_rows = lax.all_to_all(resid, ST, split_axis=0, concat_axis=1, tiled=True)
    resid_own = lax.all_to_all(resid_rows, "wid", split_axis=1, concat_axis=0, tiled=True)
    bias = lax.dynamic_slice_in_dim(
        lax.all_gather(down_bias, ST, axis=0, tiled=True), wid_index * width, width, 0
    )
    hidden_all = lax.all_gather(hidden, "wid", axis=0, tiled=True)
    down_terms = jnp.dot(hidden_all, down_weight, preferred_element_type=jnp.float32)
    down_terms = down_terms.astype(jnp.bfloat16).reshape(wid_count, st_count, rows, width)
    down_share = lax.psum_scatter(down_terms, ST, scatter_dimension=1, tiled=True)
    down_share = down_share.reshape(wid_count * rows, width).astype(jnp.float32)
    stream_own = (resid_own.astype(jnp.float32) + down_share + bias).astype(jnp.bfloat16)
    stream = lax.all_to_all(stream_own, "wid", split_axis=0, concat_axis=1, tiled=True)
    stream = lax.all_to_all(stream, ST, split_axis=1, concat_axis=0, tiled=True)
    values = stream_own.astype(jnp.float32)
    own_mean = jnp.mean(values, axis=-1, keepdims=True)
    own_m2 = jnp.sum((values - own_mean) ** 2, axis=-1, keepdims=True)
    parts = lax.all_gather(jnp.concatenate([own_mean, own_m2], axis=1), "wid")
    row_mean = jnp.mean(parts[:, :, :1], axis=0)
    row_var = (
        jnp.sum(parts[:, :, 1:], axis=0) + width * jnp.sum((parts[:, :, :1] - row_mean) ** 2, axis=0)
    ) / (width * wid_count)
    normed = ((values - row_mean) * lax.rsqrt(row_var + norm_eps) * norm_gain + norm_shift).astype(
        jnp.bfloat16
    )
    normed_all = lax.all_gather(normed, ST, axis=0, tiled=True)
    query_terms = jnp.dot(normed_all, query_weight, preferred_element_type=jnp.float32)
    query_terms = query_terms.astype(jnp.bfloat16).reshape(st_count, wid_count, rows, -1)
    share = lax.psum_scatter(query_terms, "wid", scatter_dimension=1, tiled=True)
    share = share.reshape(st_count * rows, -1)
    share = lax.all_to_all(share, ST, split_axis=0, concat_axis=1, tiled=True)
    share = lax.all_to_all(share, "wid", split_axis=1, concat_axis=0, tiled=True)
    query = (share.astype(jnp.float32) + query_bias).astype(jnp.bfloat16)
    return (stream, query.reshape(wid_count, rows, width))


def solution(mesh):
    return jax.shard_map(
        per_device,
        mesh=mesh,
        in_specs=(
            P("wid", ST),
            P("wid", ST),
            P(ST, "wid"),
            P(ST),
            P("wid"),
            P("wid"),
            P("wid", ST),
            P("wid"),
        ),
        out_specs=(P("wid", ST), P(None, ST, "wid")),
        check_vma=False,
    )
```

time: 957 us -> 615 us (0.64)
  waiting for transfers between devices: 854 us -> 400 us
  blocking collectives: 25 us -> 129 us
  starting transfers between devices: 0.2 us -> 29 us
  matrix products: 35.2 us -> 23.1 us
    all_gather x3 -> x2, waiting for transfers between devices: 622 us -> 248 us  [the longest x1 179 us: per_device(): normed_all = lax.all_gather(normed, ST, axis=0, tiled=True)]
    unnamed x6 -> x4, waiting for transfers between devices: 179 us -> 0.73 us
    all_gather x0 -> x2, blocking collectives: none -> 82.8 us  [the longest x1 72.8 us: per_device(): lax.all_gather(down_bias, ST, axis=0, tiled=True)]
    reduce_scatter x1 -> x2, waiting for transfers between devices: 52.9 us -> 124 us  [the longest x1 89.8 us: per_device(): lax.psum_scatter(down_terms, ST, scatter_dimension=1, tiled=True)]
    all_to_all x0 -> x4, starting transfers between devices: none -> 28.8 us  [the longest x1 13.2 us: per_device(): share = lax.all_to_all(share, ST, split_axis=0, concat_axis=1, tiled=True)]
    all_to_all x0 -> x4, waiting for transfers between devices: none -> 27.7 us  [the longest x1 15.2 us: per_device(): lax.all_to_all(share, 'wid', split_axis=1, concat_axis=0, tiled=True)]
    all_to_all x1 -> x2, blocking collectives: 25 us -> 46.1 us  [the longest x1 24.3 us: per_device(): lax.all_to_all(resid, ST, split_axis=0, concat_axis=1, tiled=True)]
    unnamed x18 -> x15, local copies, waits for them, and re-layouts: 17.9 us -> 1.74 us
  transfers between devices with their start and end apart: 5 -> 8, of which waited for: 5 -> 7; matrix products, arithmetic and copies ran while one was open for 1% -> 0% of each run, Pallas kernels for 0% -> 0%
where the time goes in v1:
time: 615 us; the launch traced here: 613 us
  waiting for transfers between devices  400 us (65%)
  blocking collectives  129 us (21%)
  starting transfers between devices  29 us (5%)
  matrix products  23.1 us (4%)
  between operations  13.9 us (2%)
  local copies, waits for them, and re-layouts  13.2 us (2%)
    all_gather x1, waiting for transfers between devices, per_device(): normed_all = lax.all_gather(normed, ST, axis=0, tiled=True)  179 us
    reduce_scatter x1, waiting for transfers between devices, per_device(): lax.psum_scatter(down_terms, ST, scatter_dimension=1, tiled=True)  89.8 us
    all_gather x1, blocking collectives, per_device(): lax.all_gather(down_bias, ST, axis=0, tiled=True)  72.8 us
    all_gather x1, waiting for transfers between devices, per_device(): hidden_all = lax.all_gather(hidden, 'wid', axis=0, tiled=True)  69.1 us
    reduce_scatter x1, waiting for transfers between devices, per_device(): lax.psum_scatter(query_terms, 'wid', scatter_dimension=1, tiled=True)  34.2 us
    all_to_all x1, blocking collectives, per_device(): lax.all_to_all(resid, ST, split_axis=0, concat_axis=1, tiled=True)  24.3 us
    all_to_all x1, blocking collectives, per_device(): lax.all_to_all(stream_own, 'wid', split_axis=0, concat_axis=1, tiled=True)  21.8 us
    all_to_all x1, waiting for transfers between devices, per_device(): lax.all_to_all(share, 'wid', split_axis=1, concat_axis=0, tiled=True)  15.2 us
  transfers between devices with their start and end apart: 8, of which 7 were waited for; matrix products, arithmetic and copies ran while one was open for 0% of the time, Pallas kernels for 0%

profile of v1, /device:TPU:12, one launch (start us, length us, event | category | flops | bytes accessed | tf_op | source)
XLA Modules:
  0.0 612.8 jit_solution(11373952382171088891)
XLA Ops:
  8.0 69.1 %all-gather.5.cloned.1.call-done = bf16[4096,768]{1,0:T(8,128)(2,1)} async-done(((bf16[512,768]{1,0:T(8,128)(2,1)}), bf16[4096,768]{1,0:T(8,128)(2,1)}) %all-gather.5.cloned.1.call-update) | async-done | bytes 6291472 | tf_op jit(solution)/shard_map/all_gather | solution.py:23
  77.0 13.1 %convolution_convert_fusion = bf16[4096,1536]{1,0:T(8,128)(2,1)S(1)} fusion(bf16[4096,768]{1,0:T(8,128)(2,1)} %all-gather.5.cloned.1.call-done, bf16[768,1536]{1,0:T(8,128)(2,1)S(1)} %copy-done), kind=kOutput, calls=%fused_computation | convolution fusion | flops 9669967872 | bytes 21233664 | tf_op jit(solution)/shard_map/dot_general | solution.py:24
  90.1 5.6 copy.38
  95.7 1.0 copy-done.1
  96.7 24.3 %all_to_all.90 = bf16[32,16,384]{2,1,0:T(8,128)(2,1)S(1)} all-to-all(bf16[32,16,384]{2,1,0:T(8,128)(2,1)S(1)} %bitcast.52), channel_id=1, replica_groups=mesh['section'=2,'tok'=16,'wid'=8] {'section','tok'}, dimensions={0} | all-to-all | bytes 786432 | tf_op jit(solution)/shard_map/all_to_all | solution.py:18
  122.2 3.5 all-to-all-start.1
  125.7 72.8 %all-gather.1 = f32[32,1,384]{2,1,0:T(1,128)S(1)} all-gather(f32[1,1,384]{2,1,0:T(1,128)S(1)} %reshape.121), channel_id=1, replica_groups=mesh['section'=2,'tok'=16,'wid'=8] {'section','tok'}, dimensions={0}, use_global_device_ids=true | all-gather | bytes 50688 | tf_op jit(solution)/shard_map/all_gather | solution.py:21
  198.6 89.8 %reduce-scatter.3.cloned.1.call-done = bf16[8,1,16,1536]{3,2,0,1:T(8,128)(2,1)} async-done(((bf16[8,32,16,1536]{3,2,0,1:T(8,128)(2,1)}), bf16[8,1,16,1536]{3,2,0,1:T(8,128)(2,1)}) %reduce-scatter.3.cloned.1.call-update) | async-done | bytes 393232 | tf_op jit(solution)/shard_map/reduce_scatter | solution.py:26
  288.4 1.2 convert_reduce_fusion
  290.1 10.1 %all-gather = f32[1024,2]{0,1:T(2,128)S(1)} all-gather(f32[128,2]{0,1:T(2,128)S(1)} %pad_maximum_fusion), channel_id=2, replica_groups=mesh['section'=2,'tok'=16,'wid'=8] {'wid'}, dimensions={0}, use_global_device_ids=true | all-gather | bytes 9216 | tf_op jit(solution)/shard_map/all_gather | solution.py:34
  300.2 2.0 add_convert_fusion.1
  302.3 178.7 %all-gather.7.cloned.1.call-done = bf16[4096,1536]{1,0:T(8,128)(2,1)} async-done(((bf16[128,1536]{1,0:T(8,128)(2,1)}), bf16[4096,1536]{1,0:T(8,128)(2,1)}) %all-gather.7.cloned.1.call-update) | async-done | bytes 12582928 | tf_op jit(solution)/shard_map/all_gather | solution.py:42
  481.0 10.0 %convolution_convert_fusion.1 = bf16[4096,384]{1,0:T(8,128)(2,1)S(1)} fusion(bf16[4096,1536]{1,0:T(8,128)(2,1)} %all-gather.7.cloned.1.call-done, bf16[1536,384]{1,0:T(8,128)(2,1)} %param.14), kind=kOutput, calls=%fused_computation.1 | convolution fusion | flops 4833411072 | bytes 16908288 | tf_op jit(solution)/shard_map/dot_general | solution.py:43
  491.0 2.0 copy.45
  493.0 21.8 %all_to_all.91 = bf16[8,16,1536]{2,1,0:T(8,128)(2,1)S(1)} all-to-all(bf16[8,16,1536]{2,1,0:T(8,128)(2,1)S(1)} %get-tuple-element.9), channel_id=1, replica_groups=mesh['section'=2,'tok'=16,'wid'=8] {'wid'}, dimensions={0} | all-to-all | bytes 786432 | tf_op jit(solution)/shard_map/all_to_all | solution.py:29
  514.8 34.2 %reduce-scatter.5.cloned.1.call-done = bf16[32,1,16,384]{3,2,0,1:T(8,128)(2,1)} async-done(((bf16[32,8,16,384]{3,2,0,1:T(8,128)(2,1)}), bf16[32,1,16,384]{3,2,0,1:T(8,128)(2,1)}) %reduce-scatter.5.cloned.1.call-update) | async-done | bytes 393232 | tf_op jit(solution)/shard_map/reduce_scatter | solution.py:45
  549.0 13.2 %all-to-all-start.4 = ((bf16[32,16,384]{2,1,0:T(8,128)(2,1)}), bf16[32,16,384]{2,1,0:T(8,128)(2,1)S(1)}, u32[]{:S(2)}, u32[]{:S(2)}) async-start(bf16[32,16,384]{2,1,0:T(8,128)(2,1)} %bitcast.53), calls=%async_computation.6 | async-start | bytes 786432 | tf_op jit(solution)/shard_map/all_to_all | solution.py:47
  562.7 0.9 copy.40
  563.6 6.8 %all-to-all-done.4 = bf16[32,16,384]{2,1,0:T(8,128)(2,1)S(1)} async-done(((bf16[32,16,384]{2,1,0:T(8,128)(2,1)}), bf16[32,16,384]{2,1,0:T(8,128)(2,1)S(1)}, u32[]{:S(2)}, u32[]{:S(2)}) %all-to-all-start.4) | async-done | bytes 393248 | tf_op jit(solution)/shard_map/all_to_all | solution.py:47
  570.3 7.0 %all-to-all-start.3 = ((bf16[16,32,384]{2,0,1:T(8,128)(2,1)}), bf16[16,32,384]{2,0,1:T(8,128)(2,1)S(1)}, u32[]{:S(2)}, u32[]{:S(2)}) async-start(bf16[16,32,384]{2,0,1:T(8,128)(2,1)} %copy.40), calls=%async_computation.4 | async-start | bytes 786432 | tf_op jit(solution)/shard_map/all_to_all | solution.py:30
  577.7 0.9 copy.47
  578.6 5.7 all-to-all-done.3
  584.2 5.2 all-to-all-start.5
  589.4 15.2 %all-to-all-done.5 = bf16[16,8,1536]{2,0,1:T(8,128)(2,1)S(1)} async-done(((bf16[16,8,1536]{2,0,1:T(8,128)(2,1)}), bf16[16,8,1536]{2,0,1:T(8,128)(2,1)S(1)}, u32[]{:S(2)}, u32[]{:S(2)}) %all-to-all-start.5) | async-done | bytes 393248 | tf_op jit(solution)/shard_map/all_to_all | solution.py:48
  (41 shorter events, 5.0 us)
Async XLA Ops:
  7.2 69.9 %copy-start = (bf16[768,1536]{1,0:T(8,128)(2,1)S(1)}, bf16[768,1536]{1,0:T(8,128)(2,1)}, u32[]{:S(2)}) copy-start(bf16[768,1536]{1,0:T(8,128)(2,1)} %param.10) | copy-start | bytes 7077892
  7.2 69.8 %all-gather.5.cloned.1.call-start = ((), (), s32[]{:S(2)}) async-start(), calls=%async_computation.8 | async-start | bytes 7077888 | tf_op jit(solution)/shard_map/all_gather | solution.py:23
  7.9 280.5 %reduce-scatter.3.cloned.1.call-start = ((), (), s32[]{:S(2)}) async-start(), calls=%async_computation.9 | async-start | bytes 12976128 | tf_op jit(solution)/shard_map/reduce_scatter | solution.py:26
  95.7 1.0 copy-start.1
  95.7 30.0 %copy-start.5 = (f32[384]{0:T(512)S(1)}, f32[384]{0:T(512)}, u32[]{:S(2)}) copy-start(f32[384]{0:T(512)} %param.11) | copy-start | bytes 4612
  95.7 204.5 %copy-start.2 = (f32[1536]{0:T(1024)S(1)}, f32[1536]{0:T(1024)}, u32[]{:S(2)}) copy-start(f32[1536]{0:T(1024)} %param.13) | copy-start | bytes 18436
  95.7 204.5 %copy-start.3 = (f32[1536]{0:T(1024)S(1)}, f32[1536]{0:T(1024)}, u32[]{:S(2)}) copy-start(f32[1536]{0:T(1024)} %param.12) | copy-start | bytes 18436
  122.2 76.4 %all-to-all-start.1 = ((bf16[16,8,1536]{2,0,1:T(8,128)(2,1)}), bf16[16,8,1536]{2,0,1:T(8,128)(2,1)S(1)}, u32[]{:S(2)}, u32[]{:S(2)}) async-start(bf16[16,8,1536]{2,0,1:T(8,128)(2,1)} %copy.37), calls=%async_computation.1 | async-start | bytes 786432 | tf_op jit(solution)/shard_map/all_to_all | solution.py:19
  125.7 355.3 %all-gather.7.cloned.1.call-start = ((), (), s32[]{:S(2)}) async-start(), calls=%async_computation.10 | async-start | bytes 12976128 | tf_op jit(solution)/shard_map/all_gather | solution.py:42
  302.2 246.8 %reduce-scatter.5.cloned.1.call-start = ((), (), s32[]{:S(2)}) async-start(), calls=%async_computation.11 | async-start | bytes 3538944 | tf_op jit(solution)/shard_map/reduce_scatter | solution.py:45
  493.0 111.7 %copy-start.4 = (f32[1536]{0:T(1024)S(1)}, f32[1536]{0:T(1024)}, u32[]{:S(2)}) copy-start(f32[1536]{0:T(1024)} %param.15) | copy-start | bytes 18436
  549.0 21.3 %all-to-all-start.4 = ((bf16[32,16,384]{2,1,0:T(8,128)(2,1)}), bf16[32,16,384]{2,1,0:T(8,128)(2,1)S(1)}, u32[]{:S(2)}, u32[]{:S(2)}) async-start(bf16[32,16,384]{2,1,0:T(8,128)(2,1)} %bitcast.53), calls=%async_computation.6 | async-start | bytes 786432 | tf_op jit(solution)/shard_map/all_to_all | solution.py:47
  570.3 13.9 %all-to-all-start.3 = ((bf16[16,32,384]{2,0,1:T(8,128)(2,1)}), bf16[16,32,384]{2,0,1:T(8,128)(2,1)S(1)}, u32[]{:S(2)}, u32[]{:S(2)}) async-start(bf16[16,32,384]{2,0,1:T(8,128)(2,1)} %copy.40), calls=%async_computation.4 | async-start | bytes 786432 | tf_op jit(solution)/shard_map/all_to_all | solution.py:30
  584.2 20.4 %all-to-all-start.5 = ((bf16[16,8,1536]{2,0,1:T(8,128)(2,1)}), bf16[16,8,1536]{2,0,1:T(8,128)(2,1)S(1)}, u32[]{:S(2)}, u32[]{:S(2)}) async-start(bf16[16,8,1536]{2,0,1:T(8,128)(2,1)} %copy.47), calls=%async_computation.7 | async-start | bytes 786432 | tf_op jit(solution)/shard_map/all_to_all | solution.py:48
Sparse Core Ops, SparseCore 0:
  9.8 67.1 all-gather.4
  95.9 192.5 reduce-scatter.2
  302.3 178.6 all-gather.6
  493.1 55.8 reduce-scatter.4

commit v2 on v1

--- a/solution.py
+++ b/solution.py
@@ -1,10 +1,322 @@
+import functools
+
 import jax
 import jax.numpy as jnp
 from jax import lax
+from jax.experimental import pallas as pl
+from jax.experimental.pallas import tpu as pltpu
 from jax.sharding import PartitionSpec as P
 
 norm_eps = 1e-05
 ST = ("section", "tok")
+F32, BF16 = jnp.float32, jnp.bfloat16
+MESH = pl.DeviceIdType.MESH
+UNITS = 16
+LAG = 2
+
+
+def add(*terms):
+    total = terms[0].astype(F32)
+    for term in terms[1:]:
+        total = total + term.astype(F32)
+    return total
+
+
+def place():
+    zlo, tok, wid = (lax.axis_index(name) for name in ("section", "tok", "wid"))
+    return zlo, tok // 4, tok % 4, wid // 2, wid % 2
+
+
+def down_kernel(
+    hidden, resid, bias, weight, out,
+    hbuf, rsrc, rbuf, pbuf, r1, r2, r3, r4, zs, zr, acc,
+    own_sem, ag_send, ag_recv, res_send, res_recv, rs_send, rs_recv,
+):
+    zlo, x, y, zhi, c = place()
+    tok, wid = x * 4 + y, zhi * 2 + c
+    half = hbuf.shape[3]
+    wide = weight.shape[1] // 2
+    first, second = (x, y), (y, x)
+    x_devs = [{"tok": (x + 1) % 4 * 4 + y}, {"tok": (x + 3) % 4 * 4 + y}]
+    y_devs = [{"tok": x * 4 + (y + 1) % 4}, {"tok": x * 4 + (y + 3) % 4}]
+    first_devs, second_devs = (x_devs, y_devs), (y_devs, x_devs)
+    z_devs = [{"wid": (zhi + 1) % 4 * 2 + c}, {"wid": (zhi + 3) % 4 * 2 + c}]
+    mate, pair = {"wid": zhi * 2 + 1 - c}, {"section": 1 - zlo}
+
+    def remote(src, dst, send, recv, dev):
+        return pltpu.make_async_remote_copy(src, dst, send, recv, device_id=dev, device_id_type=MESH)
+
+    res_zhi, res_c, res_zlo, res_j = zlo * 2 + x // 2, x % 2, y // 2, y % 2
+    res_wid = res_zhi * 2 + res_c
+    res_self = jnp.logical_and(res_wid == wid, res_zlo == zlo)
+    source = 4 * wid + 2 * zlo
+
+    barrier = pltpu.get_barrier_semaphore()
+    for dev in (*x_devs, *y_devs, *z_devs, mate, pair):
+        pl.semaphore_signal(barrier, inc=1, device_id=dev, device_id_type=MESH)
+
+    def greet(n, carry):
+        group = source + n // 8
+        is_self = jnp.logical_and(group == zlo * 16 + tok, n % 8 == wid)
+
+        @pl.when(jnp.logical_not(is_self))
+        def _():
+            pl.semaphore_signal(
+                barrier, inc=1, device_id=(group // 16, group % 16, n % 8), device_id_type=MESH
+            )
+        return carry
+
+    lax.fori_loop(0, 16, greet, 0)
+
+    @pl.when(res_self)
+    def _():
+        pl.semaphore_wait(barrier, 23)
+
+    @pl.when(jnp.logical_not(res_self))
+    def _():
+        pl.semaphore_wait(barrier, 24)
+
+    own_copy = pltpu.make_async_copy(hidden, hbuf.at[wid], own_sem)
+    own_copy.start()
+
+    def own_send(n):
+        h = n % 2
+        dev = (mate, *z_devs)[n // 2]
+        step = (2 + h, 4 + 4 * h, 5 + 4 * h)[n // 2]
+        return remote(hidden.at[h], hbuf.at[wid, h], ag_send.at[n], ag_recv.at[step], dev)
+
+    for n in (2, 4, 0, 3, 5, 1):
+        own_send(n).start()
+
+    def block(i):
+        g, k = i // 4, i % 4
+        mid = (g + 1) // 2 % 2
+        off = mid * (3 - 2 * (k % 2)) + 2 * (g // 3)
+        h = mid * (g - 1) + (1 - mid) * (k % 2)
+        return (zhi + off) % 4 * 2 + (c + k // 2) % 2, h
+
+    def mate_send(i):
+        w, h = block(i)
+        return remote(hbuf.at[w, h], hbuf.at[w, h], ag_send.at[8 + i], ag_recv.at[i + 2], mate)
+
+    def far_send(i, n):
+        w, h = block(i)
+        return remote(hbuf.at[w, h], hbuf.at[w, h], ag_send.at[6 + n], ag_recv.at[12 + n], z_devs[n])
+
+    rsrc[...] = (resid[...].astype(F32) + bias[...].reshape(1, 1, 1, -1)).astype(BF16)
+    narrow = resid.shape[3]
+
+    def res_copy(n, local):
+        src = rsrc.at[:, n]
+        dst = rbuf.at[:, wid, :, pl.ds(pl.multiple_of(res_j * narrow, narrow), narrow)]
+        if local:
+            return pltpu.make_async_copy(src, dst, res_recv)
+        return remote(src, dst, res_send.at[n], res_recv, (res_zlo, n, res_wid))
+
+    def res_each(n, carry):
+        is_self = jnp.logical_and(res_self, n == tok)
+
+        @pl.when(is_self)
+        def _():
+            res_copy(n, True).start()
+
+        @pl.when(jnp.logical_not(is_self))
+        def _():
+            res_copy(n, False).start()
+        return carry
+
+    lax.fori_loop(0, 16, res_each, 0)
+
+    def chunk1(i, a, d, start, size):
+        cols = pl.ds(a * wide, wide)
+        if a == 0:
+            return pbuf.at[i, d, pl.ds(start, size), :, cols]
+        return pbuf.at[i, pl.ds(start, size), d, :, cols]
+
+    def chunk2(i, a, d, start, size):
+        cols = pl.ds(a * wide + start, size)
+        if a == 0:
+            return pbuf.at[i, x, d, :, cols]
+        return pbuf.at[i, d, y, :, cols]
+
+    def hop(i, a, s, n):
+        sems = rs_send.at[i, a, s, n], rs_recv.at[i, a, s, n]
+        near = (1, 3)[n]
+        if s == 0:
+            return remote(chunk1(i, a, (first[a] + 2) % 4, 2 * n, 2), r1.at[a, i, n], *sems, first_devs[a][n])
+        if s == 1:
+            return remote(chunk1(i, a, (first[a] + near) % 4, 0, 4), r2.at[a, i, n], *sems, first_devs[a][n])
+        if s == 2:
+            src = chunk2(i, a, (second[a] + 2) % 4, n * wide // 2, wide // 2)
+            return remote(src, r3.at[a, i, n], *sems, second_devs[a][n])
+        return remote(chunk2(i, a, (second[a] + near) % 4, 0, wide), r4.at[a, i, n], *sems, second_devs[a][n])
+
+    def pair_hop(i):
+        return remote(zs.at[i], zr.at[i], rs_send.at[i, 0, 4, 0], rs_recv.at[i, 0, 4, 0], pair)
+
+    def multiply(i):
+        w, h = block(i)
+
+        @pl.when(i == 0)
+        def _():
+            own_copy.wait()
+
+        @pl.when(i >= 2)
+        def _():
+            remote(hbuf.at[w, h], hbuf.at[w, h], ag_send.at[0], ag_recv.at[i], mate).wait_recv()
+
+        @pl.when(i == 4)
+        def _():
+            far_send(i, 0).start()
+
+        @pl.when(i == 9)
+        def _():
+            far_send(i, 1).start()
+
+        @pl.when(jnp.logical_and(i >= 4, i % 4 < 2))
+        def _():
+            mate_send(i).start()
+
+        rows = hbuf[w, h]
+        for n in range(0, 2 * wide, 512):
+            part = jnp.dot(rows, weight[:, n : n + 512], preferred_element_type=F32)
+            pbuf[i, :, :, :, pl.ds(n, 512)] = part.astype(BF16).reshape(4, 4, 16, 512)
+        for a in range(2):
+            for n in range(2):
+                hop(i, a, 0, n).start()
+
+    def relay1(i):
+        for a in range(2):
+            for n in range(2):
+                hop(i, a, 0, n).wait_recv()
+                ref = chunk1(i, a, (first[a] + (1, 3)[n]) % 4, 2 * n, 2)
+                ref[...] = add(ref[...], r1[a, i, n]).astype(BF16)
+                hop(i, a, 1, n).start()
+
+    def turn(i):
+        for a in range(2):
+            for n in range(2):
+                hop(i, a, 1, n).wait_recv()
+            ref = chunk1(i, a, first[a], 0, 4)
+            ref[...] = add(ref[...], r2[a, i, 0], r2[a, i, 1]).astype(BF16)
+            for n in range(2):
+                hop(i, a, 2, n).start()
+
+    def relay2(i):
+        for a in range(2):
+            for n in range(2):
+                hop(i, a, 2, n).wait_recv()
+                ref = chunk2(i, a, (second[a] + (1, 3)[n]) % 4, n * wide // 2, wide // 2)
+                ref[...] = add(ref[...], r3[a, i, n]).astype(BF16)
+                hop(i, a, 3, n).start()
+
+    def plane_sum(i):
+        for a in range(2):
+            for n in range(2):
+                hop(i, a, 3, n).wait_recv()
+            total = add(chunk2(i, a, second[a], 0, wide)[...], r4[a, i, 0], r4[a, i, 1])
+
+            @pl.when(zlo == a)
+            def _():
+                acc[i] = total
+
+            @pl.when(zlo != a)
+            def _():
+                zs[i] = total.astype(BF16)
+                pair_hop(i).start()
+
+    def finish(i):
+        w, h = block(i)
+
+        @pl.when(i == 0)
+        def _():
+            pltpu.make_async_copy(rbuf, rbuf, res_recv).wait()
+
+        pair_hop(i).wait_recv()
+        out[h, w] = add(acc[i], zr[i], rbuf[h, w]).astype(BF16)
+
+    stages = (multiply, relay1, turn, relay2, plane_sum, finish)
+
+    def body(t, carry):
+        for n in (0, 5, 4, 3, 2, 1):
+            i = t - n * LAG
+
+            @pl.when(jnp.logical_and(i >= 0, i < UNITS))
+            def _():
+                stages[n](i)
+        return carry
+
+    lax.fori_loop(0, UNITS + 5 * LAG, body, 0)
+
+    for n in range(6):
+        own_send(n).wait_send()
+    for i in (4, 5, 8, 9, 12, 13):
+        mate_send(i).wait_send()
+    far_send(4, 0).wait_send()
+    far_send(9, 1).wait_send()
+
+    def res_done(n, carry):
+        @pl.when(jnp.logical_not(jnp.logical_and(res_self, n == tok)))
+        def _():
+            res_copy(n, False).wait_send()
+        return carry
+
+    lax.fori_loop(0, 16, res_done, 0)
+
+    def drain(i, carry):
+        for a in range(2):
+            for s in range(4):
+                for n in range(2):
+                    hop(i, a, s, n).wait_send()
+        pair_hop(i).wait_send()
+        return carry
+
+    lax.fori_loop(0, UNITS, drain, 0)
+
+
+def down(hidden, resid, bias, weight):
+    rows, depth = hidden.shape
+    width = weight.shape[1]
+    wide = width // 2
+    narrow = resid.shape[1]
+    dma = pltpu.SemaphoreType.DMA
+    return pl.pallas_call(
+        down_kernel,
+        out_shape=jax.ShapeDtypeStruct((2, 8, 16, wide), BF16),
+        in_specs=[pl.BlockSpec(memory_space=pl.ANY)] + [pl.BlockSpec(memory_space=pltpu.VMEM)] * 3,
+        out_specs=pl.BlockSpec(memory_space=pltpu.VMEM),
+        scratch_shapes=[
+            pltpu.VMEM((8, 2, rows // 2, depth), BF16),
+            pltpu.VMEM((2, 16, 16, narrow), BF16),
+            pltpu.VMEM((2, 8, 16, wide), BF16),
+            pltpu.VMEM((UNITS, 4, 4, 16, width), BF16),
+            pltpu.VMEM((2, UNITS, 2, 2, 16, wide), BF16),
+            pltpu.VMEM((2, UNITS, 2, 4, 16, wide), BF16),
+            pltpu.VMEM((2, UNITS, 2, 16, wide // 2), BF16),
+            pltpu.VMEM((2, UNITS, 2, 16, wide), BF16),
+            pltpu.VMEM((UNITS, 16, wide), BF16),
+            pltpu.VMEM((UNITS, 16, wide), BF16),
+            pltpu.VMEM((UNITS, 16, wide), F32),
+            dma,
+            dma((24,)),
+            dma((16,)),
+            dma((16,)),
+            dma,
+            dma((UNITS, 2, 5, 2)),
+            dma((UNITS, 2, 5, 2)),
+        ],
+        compiler_params=pltpu.CompilerParams(
+            collective_id=0, has_side_effects=True, vmem_limit_bytes=60 * 1024 * 1024
+        ),
+        cost_estimate=pl.CostEstimate(
+            flops=2 * 8 * rows * depth * width, bytes_accessed=2 * (rows * depth + depth * width), transcendentals=0
+        ),
+    )(
+        hidden.reshape(2, rows // 2, depth),
+        resid.reshape(2, 16, 16, narrow),
+        bias.reshape(1, narrow),
+        weight,
+    )
 
 
 def per_device(
@@ -15,17 +327,10 @@
     wid_index = lax.axis_index("wid")
     width = norm_gain.shape[0]
     rows = resid.shape[0] // st_count
-    resid_rows = lax.all_to_all(resid, ST, split_axis=0, concat_axis=1, tiled=True)
-    resid_own = lax.all_to_all(resid_rows, "wid", split_axis=1, concat_axis=0, tiled=True)
-    bias = lax.dynamic_slice_in_dim(
-        lax.all_gather(down_bias, ST, axis=0, tiled=True), wid_index * width, width, 0
-    )
-    hidden_all = lax.all_gather(hidden, "wid", axis=0, tiled=True)
-    down_terms = jnp.dot(hidden_all, down_weight, preferred_element_type=jnp.float32)
-    down_terms = down_terms.astype(jnp.bfloat16).reshape(wid_count, st_count, rows, width)
-    down_share = lax.psum_scatter(down_terms, ST, scatter_dimension=1, tiled=True)
-    down_share = down_share.reshape(wid_count * rows, width).astype(jnp.float32)
-    stream_own = (resid_own.astype(jnp.float32) + down_share + bias).astype(jnp.bfloat16)
+    down_out = down(hidden, resid, down_bias, down_weight)
+    down_out = down_out.reshape(2, wid_count * rows, width // 2)
+    stream_own = lax.all_to_all(down_out, "section", split_axis=0, concat_axis=2, tiled=True)
+    stream_own = stream_own.reshape(wid_count * rows, width)
     stream = lax.all_to_all(stream_own, "wid", split_axis=0, concat_axis=1, tiled=True)
     stream = lax.all_to_all(stream, ST, split_axis=1, concat_axis=0, tiled=True)
     values = stream_own.astype(jnp.float32)

time: 615 us -> 496 us (0.81)
  waiting for transfers between devices: 400 us -> 268 us
  Pallas kernels: 0 us -> 130 us
  blocking collectives: 129 us -> 40.7 us
  matrix products: 23.1 us -> 9.76 us
  starting transfers between devices: 29 us -> 21 us
    pallas_call x0 -> x1, Pallas kernels: none -> 130 us  [down(): pl.pallas_call(down_kernel, out_shape=jax.ShapeDtypeStruct((2, 8, 16, wid...]
    reduce_scatter x1 -> x0, waiting for transfers between devices: 89.8 us -> none  [per_device(): lax.psum_scatter(down_terms, ST, scatter_dimension=1, tiled=True)]
    all_gather x1 -> x0, blocking collectives: 72.8 us -> none  [per_device(): lax.all_gather(down_bias, ST, axis=0, tiled=True)]
    all_gather x1 -> x0, waiting for transfers between devices: 69.1 us -> none  [per_device(): hidden_all = lax.all_gather(hidden, 'wid', axis=0, tiled=True)]
    all_gather x1, waiting for transfers between devices: 179 us -> 206 us  [per_device(): normed_all = lax.all_gather(normed, ST, axis=0, tiled=True)]
    all_to_all x1, blocking collectives: 24.3 us -> 8.28 us  [per_device(): lax.all_to_all(down_out, 'section', split_axis=0, concat_axis=2, tiled=True)]
    dot_general x1 -> x0, matrix products: 13.1 us -> none  [per_device(): jnp.dot(hidden_all, down_weight, preferred_element_type=jnp.float32)]
  transfers between devices with their start and end apart: 8 -> 5, of which waited for: 7 -> 5; matrix products, arithmetic and copies ran while one was open for 0% -> 1% of each run, Pallas kernels for 0% -> 0%
where the time goes in v2:
time: 496 us; the launch traced here: 494 us
  waiting for transfers between devices  268 us (54%)
  Pallas kernels  130 us (26%)
  blocking collectives  40.7 us (8%)
  starting transfers between devices  21 us (4%)
  between operations  14.2 us (3%)
  matrix products  9.76 us (2%)
  local copies, waits for them, and re-layouts  8.53 us (2%)
    all_gather x1, waiting for transfers between devices, per_device(): normed_all = lax.all_gather(normed, ST, axis=0, tiled=True)  206 us
    pallas_call x1, Pallas kernels, down(): pl.pallas_call(down_kernel, out_shape=jax.ShapeDtypeStruct((2, 8, 16, wid...  130 us
    reduce_scatter x1, waiting for transfers between devices, per_device(): lax.psum_scatter(query_terms, 'wid', scatter_dimension=1, tiled=True)  35.3 us
    all_to_all x1, blocking collectives, per_device(): lax.all_to_all(stream_own, 'wid', split_axis=0, concat_axis=1, tiled=True)  21 us
    all_to_all x1, waiting for transfers between devices, per_device(): lax.all_to_all(share, 'wid', split_axis=1, concat_axis=0, tiled=True)  15.2 us
    all_gather x1, blocking collectives, per_device(): parts = lax.all_gather(jnp.concatenate([own_mean, own_m2], axis=1), 'wid')  11.4 us
  transfers between devices with their start and end apart: 5, of which 5 were waited for; matrix products, arithmetic and copies ran while one was open for 1% of the time, Pallas kernels for 0%

profile of v2, /device:TPU:12, one launch (start us, length us, event | category | flops | bytes accessed | tf_op | source)
XLA Modules:
  0.0 493.8 jit_solution(13302656272977560214)
XLA Ops:
  7.2 1.3 reshape.95.bias
  8.6 129.5 %shard_map.95 = bf16[2,8,16,768]{3,2,1,0:T(8,128)(2,1)} custom-call(bf16[2,256,768]{2,1,0:T(8,128)(2,1)} %bitcast.50, bf16[2,16,16,384]{3,2,1,0:T(8,128)(2,1)} %bitcast.51, f32[1,384]{1,0:T(1,128)} %reshape.95.bias, bf16[768,1536]{1,0:T(8,128)(2,1)} %weight.1), custom_call_target="tpu_custom_call" | custom-call | flops 9663676416 | bytes 3145728 | tf_op jit(solution)/shard_map/pallas_call | solution.py:283
  138.1 1.2 copy.21
  139.3 8.3 %all_to_all.79 = bf16[2,128,768]{1,2,0:T(8,128)(2,1)S(1)} all-to-all(bf16[2,128,768]{1,2,0:T(8,128)(2,1)S(1)} %copy.21), channel_id=1, replica_groups=mesh['section'=2,'tok'=16,'wid'=8] {'section'}, dimensions={0} | all-to-all | bytes 786432 | tf_op jit(solution)/shard_map/all_to_all | solution.py:332
  148.0 11.4 %all-gather = f32[1024,2]{0,1:T(2,128)S(1)} all-gather(f32[128,2]{0,1:T(2,128)S(1)} %pad_maximum_fusion), channel_id=2, replica_groups=mesh['section'=2,'tok'=16,'wid'=8] {'wid'}, dimensions={0}, use_global_device_ids=true | all-gather | bytes 9216 | tf_op jit(solution)/shard_map/all_gather | solution.py:339
  159.5 1.2 fusion.3
  160.8 206.1 %all-gather.3.cloned.1.call-done = bf16[4096,1536]{0,1:T(8,128)(2,1)} async-done(((bf16[128,1536]{0,1:T(8,128)(2,1)}), bf16[4096,1536]{0,1:T(8,128)(2,1)}) %all-gather.3.cloned.1.call-update) | async-done | bytes 12582928 | tf_op jit(solution)/shard_map/all_gather | solution.py:347
  366.9 9.8 %convolution_convert_fusion = bf16[4096,384]{1,0:T(8,128)(2,1)S(1)} fusion(bf16[4096,1536]{0,1:T(8,128)(2,1)} %all-gather.3.cloned.1.call-done, bf16[1536,384]{1,0:T(8,128)(2,1)S(1)} %copy-done), kind=kOutput, calls=%fused_computation | convolution fusion | flops 4833411072 | bytes 16908288 | tf_op jit(solution)/shard_map/dot_general | solution.py:348
  376.7 2.0 copy.25
  378.7 0.4 copy.22
  379.2 0.2 all_to_all.62
  379.4 21.0 %all_to_all.80 = bf16[8,16,1536]{2,1,0:T(8,128)(2,1)S(1)} all-to-all(bf16[8,16,1536]{2,1,0:T(8,128)(2,1)S(1)} %all_to_all.62), channel_id=1, replica_groups=mesh['section'=2,'tok'=16,'wid'=8] {'wid'}, dimensions={0} | all-to-all | bytes 786432 | tf_op jit(solution)/shard_map/all_to_all | solution.py:334
  400.5 35.3 %reduce-scatter.2.cloned.1.call-done = bf16[32,1,16,384]{3,2,0,1:T(8,128)(2,1)} async-done(((bf16[32,8,16,384]{3,2,0,1:T(8,128)(2,1)}), bf16[32,1,16,384]{3,2,0,1:T(8,128)(2,1)}) %reduce-scatter.2.cloned.1.call-update) | async-done | bytes 393232 | tf_op jit(solution)/shard_map/reduce_scatter | solution.py:350
  435.7 9.4 %all-to-all-start.3 = ((bf16[32,16,384]{2,1,0:T(8,128)(2,1)}), bf16[32,16,384]{2,1,0:T(8,128)(2,1)S(1)}, u32[]{:S(2)}, u32[]{:S(2)}) async-start(bf16[32,16,384]{2,1,0:T(8,128)(2,1)} %bitcast.44), calls=%async_computation.4 | async-start | bytes 786432 | tf_op jit(solution)/shard_map/all_to_all | solution.py:352
  445.4 0.2 all_to_all.65
  445.6 0.9 copy.24
  446.5 5.4 %all-to-all-done.3 = bf16[32,16,384]{2,1,0:T(8,128)(2,1)S(1)} async-done(((bf16[32,16,384]{2,1,0:T(8,128)(2,1)}), bf16[32,16,384]{2,1,0:T(8,128)(2,1)S(1)}, u32[]{:S(2)}, u32[]{:S(2)}) %all-to-all-start.3) | async-done | bytes 393248 | tf_op jit(solution)/shard_map/all_to_all | solution.py:352
  451.9 6.9 %all-to-all-start.2 = ((bf16[16,32,384]{2,0,1:T(8,128)(2,1)}), bf16[16,32,384]{2,0,1:T(8,128)(2,1)S(1)}, u32[]{:S(2)}, u32[]{:S(2)}) async-start(bf16[16,32,384]{2,0,1:T(8,128)(2,1)} %copy.24), calls=%async_computation.2 | async-start | bytes 786432 | tf_op jit(solution)/shard_map/all_to_all | solution.py:335
  459.1 0.9 copy.27
  460.0 5.5 %all-to-all-done.2 = bf16[16,32,384]{2,0,1:T(8,128)(2,1)S(1)} async-done(((bf16[16,32,384]{2,0,1:T(8,128)(2,1)}), bf16[16,32,384]{2,0,1:T(8,128)(2,1)S(1)}, u32[]{:S(2)}, u32[]{:S(2)}) %all-to-all-start.2) | async-done | bytes 393248 | tf_op jit(solution)/shard_map/all_to_all | solution.py:335
  465.5 4.6 all-to-all-start.4
  470.1 15.2 %all-to-all-done.4 = bf16[16,8,1536]{2,0,1:T(8,128)(2,1)S(1)} async-done(((bf16[16,8,1536]{2,0,1:T(8,128)(2,1)}), bf16[16,8,1536]{2,0,1:T(8,128)(2,1)S(1)}, u32[]{:S(2)}, u32[]{:S(2)}) %all-to-all-start.4) | async-done | bytes 393248 | tf_op jit(solution)/shard_map/all_to_all | solution.py:353
  485.4 0.8 fusion.4
  486.2 0.7 copy.32
  (24 shorter events, 1.2 us)
Async XLA Ops:
  7.2 359.8 %copy-start = (bf16[1536,384]{1,0:T(8,128)(2,1)S(1)}, bf16[1536,384]{1,0:T(8,128)(2,1)}, u32[]{:S(2)}) copy-start(bf16[1536,384]{1,0:T(8,128)(2,1)} %param.14) | copy-start | bytes 3538948
  7.2 359.7 %all-gather.3.cloned.1.call-start = ((), (), s32[]{:S(2)}) async-start(), calls=%async_computation.6 | async-start | bytes 12976128 | tf_op jit(solution)/shard_map/all_gather | solution.py:347
  8.6 151.0 %copy-start.1 = (f32[1536]{0:T(1024)S(1)}, f32[1536]{0:T(1024)}, u32[]{:S(2)}) copy-start(f32[1536]{0:T(1024)} %param.13) | copy-start | bytes 18436
  8.6 151.0 %copy-start.2 = (f32[1536]{0:T(1024)S(1)}, f32[1536]{0:T(1024)}, u32[]{:S(2)}) copy-start(f32[1536]{0:T(1024)} %param.12) | copy-start | bytes 18436
  160.8 274.9 %reduce-scatter.2.cloned.1.call-start = ((), (), s32[]{:S(2)}) async-start(), calls=%async_computation.7 | async-start | bytes 3538944 | tf_op jit(solution)/shard_map/reduce_scatter | solution.py:350
  435.7 16.2 %all-to-all-start.3 = ((bf16[32,16,384]{2,1,0:T(8,128)(2,1)}), bf16[32,16,384]{2,1,0:T(8,128)(2,1)S(1)}, u32[]{:S(2)}, u32[]{:S(2)}) async-start(bf16[32,16,384]{2,1,0:T(8,128)(2,1)} %bitcast.44), calls=%async_computation.4 | async-start | bytes 786432 | tf_op jit(solution)/shard_map/all_to_all | solution.py:352
  445.1 40.3 %copy-start.3 = (f32[1536]{0:T(1024)S(1)}, f32[1536]{0:T(1024)}, u32[]{:S(2)}) copy-start(f32[1536]{0:T(1024)} %param.15) | copy-start | bytes 18436
  451.9 13.7 %all-to-all-start.2 = ((bf16[16,32,384]{2,0,1:T(8,128)(2,1)}), bf16[16,32,384]{2,0,1:T(8,128)(2,1)S(1)}, u32[]{:S(2)}, u32[]{:S(2)}) async-start(bf16[16,32,384]{2,0,1:T(8,128)(2,1)} %copy.24), calls=%async_computation.2 | async-start | bytes 786432 | tf_op jit(solution)/shard_map/all_to_all | solution.py:335
  465.5 19.9 %all-to-all-start.4 = ((bf16[16,8,1536]{2,0,1:T(8,128)(2,1)}), bf16[16,8,1536]{2,0,1:T(8,128)(2,1)S(1)}, u32[]{:S(2)}, u32[]{:S(2)}) async-start(bf16[16,8,1536]{2,0,1:T(8,128)(2,1)} %copy.27), calls=%async_computation.5 | async-start | bytes 786432 | tf_op jit(solution)/shard_map/all_to_all | solution.py:353
Sparse Core Ops, SparseCore 0:
  160.9 205.9 all-gather.2
  378.8 56.8 reduce-scatter.1

commit v3 on v2

--- a/solution.py
+++ b/solution.py
@@ -13,6 +13,7 @@
 MESH = pl.DeviceIdType.MESH
 UNITS = 16
 LAG = 2
+LAG2 = 2
 
 
 def add(*terms):
@@ -27,10 +28,13 @@
     return zlo, tok // 4, tok % 4, wid // 2, wid % 2
 
 
-def down_kernel(
-    hidden, resid, bias, weight, out,
+def layer_kernel(
+    hidden, resid, bias, weight, gain, shift, qweight, qbias, stream, query,
     hbuf, rsrc, rbuf, pbuf, r1, r2, r3, r4, zs, zr, acc,
+    sbuf, stats, nbuf, qwm, bias2, cbuf, zbuf, fin,
     own_sem, ag_send, ag_recv, res_send, res_recv, rs_send, rs_recv,
+    qw_sem, b_sem, st_send, st_recv, so_send, so_recv, n_send, n_recv,
+    c_send, c_recv, z_send, z_recv, f_send, f_recv,
 ):
     zlo, x, y, zhi, c = place()
     tok, wid = x * 4 + y, zhi * 2 + c
@@ -51,30 +55,46 @@
     res_self = jnp.logical_and(res_wid == wid, res_zlo == zlo)
     source = 4 * wid + 2 * zlo
 
+    z = zhi * 2 + zlo
+    me = z * 2 + c
+
+    f_x, f_c = zhi % 2 * 2 + c, zhi // 2
+    f_dest = zhi == 2 * c + x // 2
+    f_self = jnp.logical_and(f_dest, c == x % 2)
+
     barrier = pltpu.get_barrier_semaphore()
-    for dev in (*x_devs, *y_devs, *z_devs, mate, pair):
-        pl.semaphore_signal(barrier, inc=1, device_id=dev, device_id_type=MESH)
-
-    def greet(n, carry):
+
+    def greet(dev, unless=None):
+        def go():
+            pl.semaphore_signal(barrier, inc=1, device_id=dev, device_id_type=MESH)
+
+        if unless is None:
+            go()
+        else:
+            pl.when(jnp.logical_not(unless))(go)
+
+    for dev in (*x_devs, *y_devs):
+        greet(dev)
+
+    def greet_each(n, carry):
         group = source + n // 8
-        is_self = jnp.logical_and(group == zlo * 16 + tok, n % 8 == wid)
-
-        @pl.when(jnp.logical_not(is_self))
-        def _():
-            pl.semaphore_signal(
-                barrier, inc=1, device_id=(group // 16, group % 16, n % 8), device_id_type=MESH
-            )
-        return carry
-
-    lax.fori_loop(0, 16, greet, 0)
-
-    @pl.when(res_self)
-    def _():
-        pl.semaphore_wait(barrier, 23)
-
-    @pl.when(jnp.logical_not(res_self))
-    def _():
-        pl.semaphore_wait(barrier, 24)
+        greet(
+            (group // 16, group % 16, n % 8),
+            jnp.logical_and(group == zlo * 16 + tok, n % 8 == wid),
+        )
+        greet((res_zlo, n, res_wid), jnp.logical_and(res_self, n == tok))
+        greet((n // 2 % 2, tok, n // 4 * 2 + n % 2), n == me)
+        return carry
+
+    lax.fori_loop(0, 16, greet_each, 0)
+    for n in range(4):
+        greet(
+            (zlo, f_x * 4 + n, zhi * 2 + f_c),
+            jnp.logical_and(jnp.logical_and(f_x == x, f_c == c), n == y),
+        )
+    met = 4 + 32 + 15 - 2 * res_self.astype(jnp.int32)
+    met = met + 16 * f_dest.astype(jnp.int32) - f_self.astype(jnp.int32)
+    pl.semaphore_wait(barrier, met)
 
     own_copy = pltpu.make_async_copy(hidden, hbuf.at[wid], own_sem)
     own_copy.start()
@@ -87,6 +107,13 @@
 
     for n in (2, 4, 0, 3, 5, 1):
         own_send(n).start()
+
+    bias2[c] = qbias[...]
+    qw_own = pltpu.make_async_copy(qweight.at[zlo], qwm.at[zlo], qw_sem.at[0])
+    qw_own.start()
+    qw_pair = remote(qweight.at[1 - zlo], qwm.at[zlo], qw_sem.at[1], qw_sem.at[2], pair)
+    bias_mate = remote(bias2.at[c], bias2.at[c], b_sem.at[0], b_sem.at[1], mate)
+    bias_mate.start()
 
     def block(i):
         g, k = i // 4, i % 4
@@ -177,6 +204,10 @@
         def _():
             mate_send(i).start()
 
+        @pl.when(i == 12)
+        def _():
+            qw_pair.start()
+
         rows = hbuf[w, h]
         for n in range(0, 2 * wide, 512):
             part = jnp.dot(rows, weight[:, n : n + 512], preferred_element_type=F32)
@@ -233,7 +264,7 @@
             pltpu.make_async_copy(rbuf, rbuf, res_recv).wait()
 
         pair_hop(i).wait_recv()
-        out[h, w] = add(acc[i], zr[i], rbuf[h, w]).astype(BF16)
+        sbuf[h, w] = add(acc[i], zr[i], rbuf[h, w]).astype(BF16)
 
     stages = (multiply, relay1, turn, relay2, plane_sum, finish)
 
@@ -247,6 +278,51 @@
         return carry
 
     lax.fori_loop(0, UNITS + 5 * LAG, body, 0)
+
+    tokens = sbuf.shape[1] * sbuf.shape[2]
+    lane = lax.broadcasted_iota(jnp.int32, (tokens, tokens), 1)
+    row = lax.broadcasted_iota(jnp.int32, (tokens, tokens), 0)
+    for q in range(2):
+        values = sbuf[q].reshape(tokens, wide).astype(F32)
+        mean = jnp.mean(values, axis=1, keepdims=True)
+        m2 = jnp.sum((values - mean) ** 2, axis=1, keepdims=True)
+        stats[me, q] = jnp.where(lane == 0, mean, m2).T[:8]
+
+    def stat_copy(n):
+        dev = (n // 2 % 2, tok, n // 4 * 2 + n % 2)
+        return remote(stats.at[me], stats.at[me], st_send.at[n], st_recv.at[me], dev)
+
+    def others(action):
+        def step(n, carry):
+            pl.when(n != me)(lambda: action(n))
+            return carry
+
+        lax.fori_loop(0, 16, step, 0)
+
+    others(lambda n: stat_copy(n).start())
+
+    def out_copy(n, local):
+        group = source + n // 8
+        src = sbuf.at[:, n % 8, :, pl.ds(pl.multiple_of(n // 8 * narrow, narrow), narrow)]
+        dst = stream.at[:, tok]
+        if local:
+            return pltpu.make_async_copy(src, dst, so_recv)
+        return remote(src, dst, so_send.at[n], so_recv, (group // 16, group % 16, n % 8))
+
+    def out_self(n):
+        return jnp.logical_and(source + n // 8 == zlo * 16 + tok, n % 8 == wid)
+
+    def out_each(n, carry):
+        @pl.when(out_self(n))
+        def _():
+            out_copy(n, True).start()
+
+        @pl.when(jnp.logical_not(out_self(n)))
+        def _():
+            out_copy(n, False).start()
+        return carry
+
+    lax.fori_loop(0, 16, out_each, 0)
 
     for n in range(6):
         own_send(n).wait_send()
@@ -274,17 +350,223 @@
     lax.fori_loop(0, UNITS, drain, 0)
 
 
-def down(hidden, resid, bias, weight):
+    def stat_wait(n):
+        here = stats.at[n]
+        remote(here, here, st_send.at[n], st_recv.at[n], mate).wait_recv()
+
+    others(stat_wait)
+    for q in range(2):
+        means, m2s = stats[:, q, 0, :], stats[:, q, 1, :]
+        mean = jnp.mean(means, axis=0, keepdims=True)
+        var = jnp.sum(m2s, axis=0, keepdims=True) + wide * jnp.sum((means - mean) ** 2, axis=0, keepdims=True)
+        scale = lax.rsqrt(var / (16 * wide) + norm_eps)
+        both = jnp.where(row == 0, mean, scale).T
+        values = sbuf[q].reshape(tokens, wide).astype(F32)
+        normed = (values - both[:, 0:1]) * both[:, 1:2] * gain[zlo] + shift[zlo]
+        nbuf[q, 0] = normed.astype(BF16)
+
+    mid = tokens // 2
+
+    def pass_on(q, u, to, slot, dev, part=None):
+        if part is None:
+            src, dst = nbuf.at[q, u], nbuf.at[q, to]
+        else:
+            rows = pl.ds(part * mid, mid)
+            src, dst = nbuf.at[q, u, rows], nbuf.at[q, to, rows]
+        return remote(src, dst, n_send.at[q, u, slot], n_recv.at[q, to, part or 0], dev)
+
+    def passes(q, u):
+        (fp, fm), (sp, sm) = first_devs[q], second_devs[q]
+        return (
+            (u == 0, lambda: pass_on(q, u, 1, 0, fp)),
+            (u == 0, lambda: pass_on(q, u, 2, 1, fm)),
+            (u == 1, lambda: pass_on(q, u, 3, 0, fp, 0)),
+            (u == 2, lambda: pass_on(q, u, 3, 1, fm, 1)),
+            (u < 4, lambda: pass_on(q, u, 4 + u, 2, sp)),
+            (u < 4, lambda: pass_on(q, u, 8 + u, 3, sm)),
+            (u // 4 == 1, lambda: pass_on(q, u, 8 + u, 2, sp, 0)),
+            (u // 4 == 2, lambda: pass_on(q, u, 4 + u, 3, sm, 1)),
+        )
+
+    def offset(e):
+        return 3 * e + 3 * (e // 2) + 2 * (e // 3)
+
+    def owned(q, u):
+        return pbuf.at[u, pl.ds(2 * q, 2), :, :, pl.ds(0, narrow)]
+
+    def given(q, u):
+        return pbuf.at[u, pl.ds(2 * q, 2), :, :, pl.ds(narrow, narrow)]
+
+    def mate_copy(q, u):
+        return remote(given(q, u), cbuf.at[q, u], c_send.at[q, u], c_recv.at[q, u], mate)
+
+    def multiply2(u):
+        for q in range(2):
+            split = jnp.logical_or(u == 3, u >= 12)
+
+            @pl.when(jnp.logical_and(u > 0, jnp.logical_not(split)))
+            def _():
+                here = nbuf.at[q, u]
+                remote(here, here, n_send.at[q, u, 0], n_recv.at[q, u, 0], mate).wait_recv()
+
+            @pl.when(split)
+            def _():
+                for part in range(2):
+                    here = nbuf.at[q, u, pl.ds(part * mid, mid)]
+                    remote(here, here, n_send.at[q, u, 0], n_recv.at[q, u, part], mate).wait_recv()
+
+            for cond, copy in passes(q, u):
+                @pl.when(cond)
+                def _():
+                    copy().start()
+
+        @pl.when(u == 0)
+        def _():
+            qw_own.wait()
+            qw_pair.wait()
+            bias_mate.wait()
+
+        for q in range(2):
+            rows = nbuf[q, u]
+            part = jnp.dot(rows, qwm[1 - c], preferred_element_type=F32)
+            given(q, u)[...] = part.astype(BF16).reshape(2, 4, 16, narrow)
+            mate_copy(q, u).start()
+            part = jnp.dot(rows, qwm[c], preferred_element_type=F32)
+            owned(q, u)[...] = part.astype(BF16).reshape(2, 4, 16, narrow)
+
+    def rel(q):
+        return (z + 16 - 2 * (2 * c + x // 2) - q) % 8
+
+    def z_copy(q, u):
+        r = rel(q)
+        far = r // 4
+        at4 = (r == 4).astype(jnp.int32)
+        down_way = at4 * (u % 2) + (1 - at4) * far
+        to = (z + 8 + 2 * down_way - 1) % 8
+        dev = (to % 2, tok, to // 2 * 2 + c)
+        return remote(owned(q, u), zbuf.at[down_way, q, u], z_send.at[q, u], z_recv.at[down_way, q, u], dev)
+
+    def z_wait(q, u, side):
+        here = zbuf.at[side, q, u]
+        remote(here, here, z_send.at[q, u], z_recv.at[side, q, u], mate).wait_recv()
+
+    def fin_copy(q, u, local):
+        one, two = offset(u % 4), offset(u // 4)
+        to = ((x + one) % 4 * 4 + (y + two) % 4, (x + two) % 4 * 4 + (y + one) % 4)[q]
+        dst = query.at[:, :, pl.ds(pl.multiple_of(y * narrow, narrow), narrow)]
+        if local:
+            return pltpu.make_async_copy(fin.at[u], dst, f_recv.at[y])
+        return remote(fin.at[u], dst, f_send.at[u], f_recv.at[y], (zlo, to, zhi * 2 + x % 2))
+
+    def relay(q, u):
+        r = rel(q)
+        here = owned(q, u)
+        mate_copy(q, u).wait_recv()
+        side = r // 4
+        takes = jnp.logical_or(
+            jnp.logical_or(r == 1, r == 2),
+            jnp.logical_or(r >= 6, jnp.logical_or(
+                jnp.logical_and(r == 3, u % 2 == 0), jnp.logical_and(r == 5, u % 2 == 1)
+            )),
+        )
+
+        @pl.when(takes)
+        def _():
+            z_wait(q, u, side)
+            here[...] = add(here[...], cbuf[q, u], zbuf[side, q, u]).astype(BF16)
+
+        @pl.when(jnp.logical_and(jnp.logical_not(takes), r != 0))
+        def _():
+            here[...] = add(here[...], cbuf[q, u]).astype(BF16)
+
+        @pl.when(r != 0)
+        def _():
+            z_copy(q, u).start()
+
+        @pl.when(r == 0)
+        def _():
+            z_wait(q, u, 0)
+            z_wait(q, u, 1)
+            total = add(here[...], cbuf[q, u], zbuf[0, q, u], zbuf[1, q, u]).reshape(8, 16, narrow)
+            fin[u] = (total + bias2[x % 2, y][0:1].reshape(1, 1, narrow)).astype(BF16)
+            self_too = jnp.logical_and(u == 0, f_self)
+
+            @pl.when(self_too)
+            def _():
+                fin_copy(q, u, True).start()
+
+            @pl.when(jnp.logical_not(self_too))
+            def _():
+                fin_copy(q, u, False).start()
+
+    def body2(t, carry):
+        @pl.when(t < UNITS)
+        def _():
+            multiply2(t)
+
+        for q in range(2):
+            r = rel(q)
+            u = t - LAG2 * (1 + (r - 4) * (2 * (r // 4) - 1))
+
+            @pl.when(jnp.logical_and(u >= 0, u < UNITS))
+            def _():
+                relay(q, u)
+        return carry
+
+    lax.fori_loop(0, UNITS + 5 * LAG2, body2, 0)
+
+    pltpu.make_async_copy(stream, stream, so_recv).wait()
+    for n in range(4):
+        dst = query.at[:, :, pl.ds(n * narrow, narrow)]
+        pltpu.make_async_copy(dst, dst, f_recv.at[n]).wait()
+    others(lambda n: stat_copy(n).wait_send())
+
+    def out_done(n, carry):
+        @pl.when(jnp.logical_not(out_self(n)))
+        def _():
+            out_copy(n, False).wait_send()
+        return carry
+
+    lax.fori_loop(0, 16, out_done, 0)
+
+    def drain2(u, carry):
+        for q in range(2):
+            for cond, copy in passes(q, u):
+                @pl.when(cond)
+                def _():
+                    copy().wait_send()
+            mate_copy(q, u).wait_send()
+
+            @pl.when(rel(q) != 0)
+            def _():
+                z_copy(q, u).wait_send()
+
+            @pl.when(jnp.logical_and(rel(q) == 0, jnp.logical_not(jnp.logical_and(u == 0, f_self))))
+            def _():
+                fin_copy(q, u, False).wait_send()
+        return carry
+
+    lax.fori_loop(0, UNITS, drain2, 0)
+
+
+def per_device(
+    hidden, resid, down_weight, down_bias, norm_gain, norm_shift, query_weight, query_bias
+):
     rows, depth = hidden.shape
-    width = weight.shape[1]
+    width = down_weight.shape[1]
     wide = width // 2
     narrow = resid.shape[1]
     dma = pltpu.SemaphoreType.DMA
-    return pl.pallas_call(
-        down_kernel,
-        out_shape=jax.ShapeDtypeStruct((2, 8, 16, wide), BF16),
-        in_specs=[pl.BlockSpec(memory_space=pl.ANY)] + [pl.BlockSpec(memory_space=pltpu.VMEM)] * 3,
-        out_specs=pl.BlockSpec(memory_space=pltpu.VMEM),
+    vmem = pl.BlockSpec(memory_space=pltpu.VMEM)
+    hbm = pl.BlockSpec(memory_space=pl.ANY)
+    stream, query = pl.pallas_call(
+        layer_kernel,
+        out_shape=(
+            jax.ShapeDtypeStruct((2, 16, 16, narrow), BF16),
+            jax.ShapeDtypeStruct((8, 16, width), BF16),
+        ),
+        in_specs=[hbm, vmem, vmem, vmem, vmem, vmem, hbm, vmem],
+        out_specs=(vmem, vmem),
         scratch_shapes=[
             pltpu.VMEM((8, 2, rows // 2, depth), BF16),
             pltpu.VMEM((2, 16, 16, narrow), BF16),
@@ -297,6 +579,14 @@
             pltpu.VMEM((UNITS, 16, wide), BF16),
             pltpu.VMEM((UNITS, 16, wide), BF16),
             pltpu.VMEM((UNITS, 16, wide), F32),
+            pltpu.VMEM((2, 8, 16, wide), BF16),
+            pltpu.VMEM((16, 2, 8, 128), F32),
+            pltpu.VMEM((2, UNITS, 128, wide), BF16),
+            pltpu.VMEM((2, wide, narrow), BF16),
+            pltpu.VMEM((2, 4, 8, narrow), F32),
+            pltpu.VMEM((2, UNITS, 2, 4, 16, narrow), BF16),
+            pltpu.VMEM((2, 2, UNITS, 2, 4, 16, narrow), BF16),
+            pltpu.VMEM((UNITS, 8, 16, narrow), BF16),
             dma,
             dma((24,)),
             dma((16,)),
@@ -304,55 +594,40 @@
             dma,
             dma((UNITS, 2, 5, 2)),
             dma((UNITS, 2, 5, 2)),
+            dma((3,)),
+            dma((2,)),
+            dma((16,)),
+            dma((16,)),
+            dma((16,)),
+            dma,
+            dma((2, UNITS, 4)),
+            dma((2, UNITS, 2)),
+            dma((2, UNITS)),
+            dma((2, UNITS)),
+            dma((2, UNITS)),
+            dma((2, 2, UNITS)),
+            dma((UNITS,)),
+            dma((4,)),
         ],
         compiler_params=pltpu.CompilerParams(
-            collective_id=0, has_side_effects=True, vmem_limit_bytes=60 * 1024 * 1024
+            collective_id=0, has_side_effects=True, vmem_limit_bytes=62 * 1024 * 1024
         ),
         cost_estimate=pl.CostEstimate(
-            flops=2 * 8 * rows * depth * width, bytes_accessed=2 * (rows * depth + depth * width), transcendentals=0
+            flops=16 * rows * depth * width + 16 * rows * wide * wide,
+            bytes_accessed=2 * (rows * depth + depth * width),
+            transcendentals=0,
         ),
     )(
         hidden.reshape(2, rows // 2, depth),
         resid.reshape(2, 16, 16, narrow),
-        bias.reshape(1, narrow),
-        weight,
+        down_bias.reshape(1, narrow),
+        down_weight,
+        norm_gain.reshape(2, 1, wide),
+        norm_shift.reshape(2, 1, wide),
+        query_weight.reshape(2, wide, narrow),
+        jnp.broadcast_to(query_bias.reshape(4, 1, narrow), (4, 8, narrow)),
     )
-
-
-def per_device(
-    hidden, resid, down_weight, down_bias, norm_gain, norm_shift, query_weight, query_bias
-):
-    wid_count = lax.axis_size("wid")
-    st_count = lax.axis_size("section") * lax.axis_size("tok")
-    wid_index = lax.axis_index("wid")
-    width = norm_gain.shape[0]
-    rows = resid.shape[0] // st_count
-    down_out = down(hidden, resid, down_bias, down_weight)
-    down_out = down_out.reshape(2, wid_count * rows, width // 2)
-    stream_own = lax.all_to_all(down_out, "section", split_axis=0, concat_axis=2, tiled=True)
-    stream_own = stream_own.reshape(wid_count * rows, width)
-    stream = lax.all_to_all(stream_own, "wid", split_axis=0, concat_axis=1, tiled=True)
-    stream = lax.all_to_all(stream, ST, split_axis=1, concat_axis=0, tiled=True)
-    values = stream_own.astype(jnp.float32)
-    own_mean = jnp.mean(values, axis=-1, keepdims=True)
-    own_m2 = jnp.sum((values - own_mean) ** 2, axis=-1, keepdims=True)
-    parts = lax.all_gather(jnp.concatenate([own_mean, own_m2], axis=1), "wid")
-    row_mean = jnp.mean(parts[:, :, :1], axis=0)
-    row_var = (
-        jnp.sum(parts[:, :, 1:], axis=0) + width * jnp.sum((parts[:, :, :1] - row_mean) ** 2, axis=0)
-    ) / (width * wid_count)
-    normed = ((values - row_mean) * lax.rsqrt(row_var + norm_eps) * norm_gain + norm_shift).astype(
-        jnp.bfloat16
-    )
-    normed_all = lax.all_gather(normed, ST, axis=0, tiled=True)
-    query_terms = jnp.dot(normed_all, query_weight, preferred_element_type=jnp.float32)
-    query_terms = query_terms.astype(jnp.bfloat16).reshape(st_count, wid_count, rows, -1)
-    share = lax.psum_scatter(query_terms, "wid", scatter_dimension=1, tiled=True)
-    share = share.reshape(st_count * rows, -1)
-    share = lax.all_to_all(share, ST, split_axis=0, concat_axis=1, tiled=True)
-    share = lax.all_to_all(share, "wid", split_axis=1, concat_axis=0, tiled=True)
-    query = (share.astype(jnp.float32) + query_bias).astype(jnp.bfloat16)
-    return (stream, query.reshape(wid_count, rows, width))
+    return (stream.reshape(rows, narrow), query)
 
 
 def solution(mesh):

time: 496 us -> 236 us (0.48)
  waiting for transfers between devices: 268 us -> 0 us
  Pallas kernels: 130 us -> 224 us
  blocking collectives: 40.7 us -> 0 us
  starting transfers between devices: 21 us -> 0 us
  between operations: 14.2 us -> 0.64 us
  matrix products: 9.76 us -> 0 us
    all_gather x1 -> x0, waiting for transfers between devices: 206 us -> none  [per_device(): normed_all = lax.all_gather(normed, ST, axis=0, tiled=True)]
    pallas_call x1, Pallas kernels: 130 us -> 224 us  [per_device(): pl.pallas_call(layer_kernel, out_shape=(jax.ShapeDtypeStruct((2, 16, 16,...]
    reduce_scatter x1 -> x0, waiting for transfers between devices: 35.3 us -> none  [per_device(): lax.psum_scatter(query_terms, 'wid', scatter_dimension=1, tiled=True)]
    all_to_all x2 -> x0, blocking collectives: 29.3 us -> none  [the longest x1 21 us: per_device(): lax.all_to_all(stream_own, 'wid', split_axis=0, concat_axis=1, tiled=True)]
    all_to_all x3 -> x0, waiting for transfers between devices: 26.2 us -> none  [the longest x1 15.2 us: per_device(): lax.all_to_all(share, 'wid', split_axis=1, concat_axis=0, tiled=True)]
    all_to_all x3 -> x0, starting transfers between devices: 20.9 us -> none  [the longest x1 9.4 us: per_device(): share = lax.all_to_all(share, ST, split_axis=0, concat_axis=1, tiled=True)]
    all_gather x1 -> x0, blocking collectives: 11.4 us -> none  [per_device(): parts = lax.all_gather(jnp.concatenate([own_mean, own_m2], axis=1), 'wid')]
    dot_general x1 -> x0, matrix products: 9.76 us -> none  [per_device(): jnp.dot(normed_all, query_weight, preferred_element_type=jnp.float32)]
  transfers between devices with their start and end apart: 5 -> 0, of which waited for: 5 -> 0; matrix products, arithmetic and copies ran while one was open for 1% -> 0% of each run, Pallas kernels for 0% -> 0%
where the time goes in v3:
time: 236 us; the launch traced here: 234 us
  Pallas kernels  224 us (95%)
  local copies, waits for them, and re-layouts  8.72 us (4%)
    pallas_call x1, Pallas kernels, per_device(): pl.pallas_call(layer_kernel, out_shape=(jax.ShapeDtypeStruct((2, 16, 16,...  224 us

profile of v3, /device:TPU:12, one launch (start us, length us, event | category | flops | bytes accessed | tf_op | source)
XLA Modules:
  0.0 233.8 jit_solution(5635350004344683375)
XLA Ops:
  0.6 1.2 reshape.29.bias
  1.9 1.3 reshape.30.gain
  3.2 1.3 reshape.31.shift
  4.5 0.7 broadcast_in_dim.7
  5.2 0.6 broadcast_in_dim.8.qbias
  5.8 224.4 %shard_map.95 = (bf16[2,16,16,384]{3,2,1,0:T(8,128)(2,1)}, bf16[8,16,1536]{2,1,0:T(8,128)(2,1)}) custom-call(bf16[2,256,768]{2,1,0:T(8,128)(2,1)} %bitcast.6, bf16[2,16,16,384]{3,2,1,0:T(8,128)(2,1)} %bitcast.7, f32[1,384]{1,0:T(1,128)} %reshape.29.bias, bf16[768,1536]{1,0:T(8,128)(2,1)} %weight.1, f32[2,1,768]{2,1,0:T(1,128)} %reshape.30.gain, ...), custom_call_target="tpu_custom_call" | custom-call | flops 14495514624 | bytes 3145728 | tf_op jit(solution)/shard_map/pallas_call | solution.py:562
  230.2 1.8 copy.12
  232.0 1.8 copy.13

commit v4 on v3

--- a/solution.py
+++ b/solution.py
@@ -13,7 +13,14 @@
 MESH = pl.DeviceIdType.MESH
 UNITS = 16
 LAG = 2
+BEAT = 6
+ORDER = (0, 4, 3, 2, 1)
+PACE = True
+LOOK = 1
+WALK = (0, 1, 2, 4, 8, 3, 5, 9, 6, 10, 12, 7, 11, 13, 14, 15)
 LAG2 = 2
+OUT_AT = 0
+EARLY = True
 
 
 def add(*terms):
@@ -30,7 +37,7 @@
 
 def layer_kernel(
     hidden, resid, bias, weight, gain, shift, qweight, qbias, stream, query,
-    hbuf, rsrc, rbuf, pbuf, r1, r2, r3, r4, zs, zr, acc,
+    hbuf, rsrc, rmid, rbuf, pbuf, r1, r2, r3, r4, zs, zr, acc,
     sbuf, stats, nbuf, qwm, bias2, cbuf, zbuf, fin,
     own_sem, ag_send, ag_recv, res_send, res_recv, rs_send, rs_recv,
     qw_sem, b_sem, st_send, st_recv, so_send, so_recv, n_send, n_recv,
@@ -50,54 +57,35 @@
     def remote(src, dst, send, recv, dev):
         return pltpu.make_async_remote_copy(src, dst, send, recv, device_id=dev, device_id_type=MESH)
 
-    res_zhi, res_c, res_zlo, res_j = zlo * 2 + x // 2, x % 2, y // 2, y % 2
-    res_wid = res_zhi * 2 + res_c
-    res_self = jnp.logical_and(res_wid == wid, res_zlo == zlo)
     source = 4 * wid + 2 * zlo
-
     z = zhi * 2 + zlo
     me = z * 2 + c
 
-    f_x, f_c = zhi % 2 * 2 + c, zhi // 2
-    f_dest = zhi == 2 * c + x // 2
-    f_self = jnp.logical_and(f_dest, c == x % 2)
+    f_self = jnp.logical_and(zhi == 2 * c + x // 2, c == x % 2)
 
     barrier = pltpu.get_barrier_semaphore()
 
-    def greet(dev, unless=None):
-        def go():
-            pl.semaphore_signal(barrier, inc=1, device_id=dev, device_id_type=MESH)
-
-        if unless is None:
-            go()
-        else:
-            pl.when(jnp.logical_not(unless))(go)
+    def greet(dev):
+        pl.semaphore_signal(barrier, inc=1, device_id=dev, device_id_type=MESH)
 
     for dev in (*x_devs, *y_devs):
         greet(dev)
 
-    def greet_each(n, carry):
-        group = source + n // 8
-        greet(
-            (group // 16, group % 16, n % 8),
-            jnp.logical_and(group == zlo * 16 + tok, n % 8 == wid),
-        )
-        greet((res_zlo, n, res_wid), jnp.logical_and(res_self, n == tok))
-        greet((n // 2 % 2, tok, n // 4 * 2 + n % 2), n == me)
+    def greet_line(n, carry):
+        pl.when(n != me)(lambda: greet((n // 2 % 2, tok, n // 4 * 2 + n % 2)))
         return carry
 
-    lax.fori_loop(0, 16, greet_each, 0)
-    for n in range(4):
-        greet(
-            (zlo, f_x * 4 + n, zhi * 2 + f_c),
-            jnp.logical_and(jnp.logical_and(f_x == x, f_c == c), n == y),
-        )
-    met = 4 + 32 + 15 - 2 * res_self.astype(jnp.int32)
-    met = met + 16 * f_dest.astype(jnp.int32) - f_self.astype(jnp.int32)
-    pl.semaphore_wait(barrier, met)
+    lax.fori_loop(0, 16, greet_line, 0)
 
     own_copy = pltpu.make_async_copy(hidden, hbuf.at[wid], own_sem)
     own_copy.start()
+    qw_own = pltpu.make_async_copy(qweight.at[zlo], qwm.at[zlo], qw_sem.at[0])
+    qw_own.start()
+    narrow = resid.shape[3]
+    rsrc[...] = (resid[...].astype(F32) + bias[...].reshape(1, 1, 1, -1)).astype(BF16)
+    for n in range(4):
+        bias2[c, n] = jnp.broadcast_to(qbias[n * narrow : (n + 1) * narrow].reshape(1, narrow), (8, narrow))
+    pl.semaphore_wait(barrier, 4 + 15)
 
     def own_send(n):
         h = n % 2
@@ -105,12 +93,9 @@
         step = (2 + h, 4 + 4 * h, 5 + 4 * h)[n // 2]
         return remote(hidden.at[h], hbuf.at[wid, h], ag_send.at[n], ag_recv.at[step], dev)
 
-    for n in (2, 4, 0, 3, 5, 1):
+    for n in (2, 4, 0, 1) if PACE else (2, 4, 0, 3, 5, 1):
         own_send(n).start()
 
-    bias2[c] = qbias[...]
-    qw_own = pltpu.make_async_copy(qweight.at[zlo], qwm.at[zlo], qw_sem.at[0])
-    qw_own.start()
     qw_pair = remote(qweight.at[1 - zlo], qwm.at[zlo], qw_sem.at[1], qw_sem.at[2], pair)
     bias_mate = remote(bias2.at[c], bias2.at[c], b_sem.at[0], b_sem.at[1], mate)
     bias_mate.start()
@@ -130,29 +115,34 @@
         w, h = block(i)
         return remote(hbuf.at[w, h], hbuf.at[w, h], ag_send.at[6 + n], ag_recv.at[12 + n], z_devs[n])
 
-    rsrc[...] = (resid[...].astype(F32) + bias[...].reshape(1, 1, 1, -1)).astype(BF16)
-    narrow = resid.shape[3]
-
     def res_copy(n, local):
-        src = rsrc.at[:, n]
-        dst = rbuf.at[:, wid, :, pl.ds(pl.multiple_of(res_j * narrow, narrow), narrow)]
+        src, dst = rsrc.at[:, n], rmid.at[tok]
         if local:
-            return pltpu.make_async_copy(src, dst, res_recv)
-        return remote(src, dst, res_send.at[n], res_recv, (res_zlo, n, res_wid))
-
-    def res_each(n, carry):
-        is_self = jnp.logical_and(res_self, n == tok)
-
-        @pl.when(is_self)
-        def _():
-            res_copy(n, True).start()
-
-        @pl.when(jnp.logical_not(is_self))
-        def _():
-            res_copy(n, False).start()
-        return carry
-
-    lax.fori_loop(0, 16, res_each, 0)
+            return pltpu.make_async_copy(src, dst, res_recv.at[0])
+        return remote(src, dst, res_send.at[0], res_recv.at[0], (zlo, n, wid))
+
+    def res_start(n):
+        pl.when(n == tok)(lambda: res_copy(n, True).start())
+        pl.when(n != tok)(lambda: res_copy(n, False).start())
+
+    def res_line(n, local):
+        src, dst = rmid.at[pl.ds(2 * n, 2)], rbuf.at[wid]
+        if local:
+            return pltpu.make_async_copy(src, dst, res_recv.at[1])
+        dev = (n % 2, tok, (zlo * 2 + n // 4) * 2 + n // 2 % 2)
+        return remote(src, dst, res_send.at[1], res_recv.at[1], dev)
+
+    def res_turn():
+        sent(rmid, res_recv.at[0])
+        for n in range(8):
+            same = jnp.logical_and(
+                n % 2 == zlo, jnp.logical_and(zlo * 2 + n // 4 == zhi, n // 2 % 2 == c)
+            )
+            pl.when(same)(lambda: res_line(n, True).start())
+            pl.when(jnp.logical_not(same))(lambda: res_line(n, False).start())
+
+    def sent(ref, sem):
+        pltpu.make_async_copy(ref, ref, sem).wait()
 
     def chunk1(i, a, d, start, size):
         cols = pl.ds(a * wide, wide)
@@ -167,7 +157,7 @@
         return pbuf.at[i, d, y, :, cols]
 
     def hop(i, a, s, n):
-        sems = rs_send.at[i, a, s, n], rs_recv.at[i, a, s, n]
+        sems = rs_send.at[a, s], rs_recv.at[i, a, s, n]
         near = (1, 3)[n]
         if s == 0:
             return remote(chunk1(i, a, (first[a] + 2) % 4, 2 * n, 2), r1.at[a, i, n], *sems, first_devs[a][n])
@@ -179,7 +169,7 @@
         return remote(chunk2(i, a, (second[a] + near) % 4, 0, wide), r4.at[a, i, n], *sems, second_devs[a][n])
 
     def pair_hop(i):
-        return remote(zs.at[i], zr.at[i], rs_send.at[i, 0, 4, 0], rs_recv.at[i, 0, 4, 0], pair)
+        return remote(zs.at[i], zr.at[i], rs_send.at[0, 4], rs_recv.at[i, 0, 4, 0], pair)
 
     def multiply(i):
         w, h = block(i)
@@ -192,21 +182,20 @@
         def _():
             remote(hbuf.at[w, h], hbuf.at[w, h], ag_send.at[0], ag_recv.at[i], mate).wait_recv()
 
-        @pl.when(i == 4)
-        def _():
-            far_send(i, 0).start()
-
-        @pl.when(i == 9)
-        def _():
-            far_send(i, 1).start()
+        copies = ((8, far_send(4, 0)), (9, far_send(9, 1)))
+        if PACE:
+            copies = ((4, own_send(3)), (5, own_send(5)), *copies)
+        else:
+            copies = ((4, far_send(4, 0)), (9, far_send(9, 1)))
+        for step, copy in copies:
+            pl.when(i == step)(copy.start)
 
         @pl.when(jnp.logical_and(i >= 4, i % 4 < 2))
         def _():
             mate_send(i).start()
 
-        @pl.when(i == 12)
-        def _():
-            qw_pair.start()
+        pl.when(i == 12)(res_turn)
+        pl.when(i == 13)(qw_pair.start)
 
         rows = hbuf[w, h]
         for n in range(0, 2 * wide, 512):
@@ -249,7 +238,8 @@
 
             @pl.when(zlo == a)
             def _():
-                acc[i] = total
+                w, h = block(i)
+                acc[h, w] = total
 
             @pl.when(zlo != a)
             def _():
@@ -258,26 +248,40 @@
 
     def finish(i):
         w, h = block(i)
-
-        @pl.when(i == 0)
-        def _():
-            pltpu.make_async_copy(rbuf, rbuf, res_recv).wait()
-
         pair_hop(i).wait_recv()
-        sbuf[h, w] = add(acc[i], zr[i], rbuf[h, w]).astype(BF16)
-
-    stages = (multiply, relay1, turn, relay2, plane_sum, finish)
+        acc[h, w] = add(acc[h, w], zr[i])
+
+    stages = (multiply, relay1, turn, relay2, plane_sum)
 
     def body(t, carry):
-        for n in (0, 5, 4, 3, 2, 1):
-            i = t - n * LAG
-
-            @pl.when(jnp.logical_and(i >= 0, i < UNITS))
+        for n in ORDER:
+            turn_at = t - n * LAG
+            i = turn_at // BEAT * 4 + turn_at % BEAT
+            due = jnp.logical_and(turn_at % BEAT < 4, i < UNITS)
+
+            @pl.when(jnp.logical_and(turn_at >= 0, due))
             def _():
                 stages[n](i)
+
+        @pl.when(jnp.logical_and(t > 4 * LAG, t < 4 * LAG + 5))
+        def _():
+            for n in range(4):
+                res_start(4 * (t - 4 * LAG - 1) + n)
         return carry
 
-    lax.fori_loop(0, UNITS + 5 * LAG, body, 0)
+    lax.fori_loop(0, 3 * BEAT + 4 + 4 * LAG, body, 0)
+
+    def finish_each(i, carry):
+        finish(i)
+        return carry
+
+    lax.fori_loop(0, UNITS, finish_each, 0)
+
+    sent(rbuf, res_recv.at[1])
+    for q in range(2):
+        for n in range(2):
+            cols = pl.ds(n * narrow, narrow)
+            sbuf[q, :, :, cols] = add(acc[q, :, :, cols], rbuf[:, n, q]).astype(BF16)
 
     tokens = sbuf.shape[1] * sbuf.shape[2]
     lane = lax.broadcasted_iota(jnp.int32, (tokens, tokens), 1)
@@ -290,7 +294,7 @@
 
     def stat_copy(n):
         dev = (n // 2 % 2, tok, n // 4 * 2 + n % 2)
-        return remote(stats.at[me], stats.at[me], st_send.at[n], st_recv.at[me], dev)
+        return remote(stats.at[me], stats.at[me], st_send, st_recv.at[me], dev)
 
     def others(action):
         def step(n, carry):
@@ -307,22 +311,14 @@
         dst = stream.at[:, tok]
         if local:
             return pltpu.make_async_copy(src, dst, so_recv)
-        return remote(src, dst, so_send.at[n], so_recv, (group // 16, group % 16, n % 8))
+        return remote(src, dst, so_send, so_recv, (group // 16, group % 16, n % 8))
 
     def out_self(n):
         return jnp.logical_and(source + n // 8 == zlo * 16 + tok, n % 8 == wid)
 
-    def out_each(n, carry):
-        @pl.when(out_self(n))
-        def _():
-            out_copy(n, True).start()
-
-        @pl.when(jnp.logical_not(out_self(n)))
-        def _():
-            out_copy(n, False).start()
-        return carry
-
-    lax.fori_loop(0, 16, out_each, 0)
+    def out_start(n):
+        pl.when(out_self(n))(lambda: out_copy(n, True).start())
+        pl.when(jnp.logical_not(out_self(n)))(lambda: out_copy(n, False).start())
 
     for n in range(6):
         own_send(n).wait_send()
@@ -331,30 +327,19 @@
     far_send(4, 0).wait_send()
     far_send(9, 1).wait_send()
 
-    def res_done(n, carry):
-        @pl.when(jnp.logical_not(jnp.logical_and(res_self, n == tok)))
-        def _():
-            res_copy(n, False).wait_send()
-        return carry
-
-    lax.fori_loop(0, 16, res_done, 0)
-
-    def drain(i, carry):
-        for a in range(2):
-            for s in range(4):
-                for n in range(2):
-                    hop(i, a, s, n).wait_send()
-        pair_hop(i).wait_send()
-        return carry
-
-    lax.fori_loop(0, UNITS, drain, 0)
-
+    for a in range(2):
+        for n, ref in enumerate((r1, r2, r3, r4)):
+            sent(ref.at[a], rs_send.at[a, n])
+    sent(zr, rs_send.at[0, 4])
 
     def stat_wait(n):
         here = stats.at[n]
-        remote(here, here, st_send.at[n], st_recv.at[n], mate).wait_recv()
+        remote(here, here, st_send, st_recv.at[n], mate).wait_recv()
 
     others(stat_wait)
+    gains, shifts = (
+        jnp.where(zlo == 0, ref[0:wide], ref[wide : 2 * wide]).reshape(1, wide) for ref in (gain, shift)
+    )
     for q in range(2):
         means, m2s = stats[:, q, 0, :], stats[:, q, 1, :]
         mean = jnp.mean(means, axis=0, keepdims=True)
@@ -362,30 +347,30 @@
         scale = lax.rsqrt(var / (16 * wide) + norm_eps)
         both = jnp.where(row == 0, mean, scale).T
         values = sbuf[q].reshape(tokens, wide).astype(F32)
-        normed = (values - both[:, 0:1]) * both[:, 1:2] * gain[zlo] + shift[zlo]
+        normed = (values - both[:, 0:1]) * both[:, 1:2] * gains + shifts
         nbuf[q, 0] = normed.astype(BF16)
 
     mid = tokens // 2
 
-    def pass_on(q, u, to, slot, dev, part=None):
+    def pass_on(q, u, to, dev, part=None):
         if part is None:
             src, dst = nbuf.at[q, u], nbuf.at[q, to]
         else:
             rows = pl.ds(part * mid, mid)
             src, dst = nbuf.at[q, u, rows], nbuf.at[q, to, rows]
-        return remote(src, dst, n_send.at[q, u, slot], n_recv.at[q, to, part or 0], dev)
+        return remote(src, dst, n_send.at[q], n_recv.at[q, to, part or 0], dev)
 
     def passes(q, u):
         (fp, fm), (sp, sm) = first_devs[q], second_devs[q]
         return (
-            (u == 0, lambda: pass_on(q, u, 1, 0, fp)),
-            (u == 0, lambda: pass_on(q, u, 2, 1, fm)),
-            (u == 1, lambda: pass_on(q, u, 3, 0, fp, 0)),
-            (u == 2, lambda: pass_on(q, u, 3, 1, fm, 1)),
-            (u < 4, lambda: pass_on(q, u, 4 + u, 2, sp)),
-            (u < 4, lambda: pass_on(q, u, 8 + u, 3, sm)),
-            (u // 4 == 1, lambda: pass_on(q, u, 8 + u, 2, sp, 0)),
-            (u // 4 == 2, lambda: pass_on(q, u, 4 + u, 3, sm, 1)),
+            (u == 0, lambda: pass_on(q, u, 1, fp)),
+            (u == 0, lambda: pass_on(q, u, 2, fm)),
+            (u == 1, lambda: pass_on(q, u, 3, fp, 0)),
+            (u == 2, lambda: pass_on(q, u, 3, fm, 1)),
+            (u < 4, lambda: pass_on(q, u, 4 + u, sp)),
+            (u < 4, lambda: pass_on(q, u, 8 + u, sm)),
+            (u // 4 == 1, lambda: pass_on(q, u, 8 + u, sp, 0)),
+            (u // 4 == 2, lambda: pass_on(q, u, 4 + u, sm, 1)),
         )
 
     def offset(e):
@@ -398,29 +383,42 @@
         return pbuf.at[u, pl.ds(2 * q, 2), :, :, pl.ds(narrow, narrow)]
 
     def mate_copy(q, u):
-        return remote(given(q, u), cbuf.at[q, u], c_send.at[q, u], c_recv.at[q, u], mate)
-
-    def multiply2(u):
+        return remote(given(q, u), cbuf.at[q, u], c_send.at[q], c_recv.at[q, u], mate)
+
+    def walk(k):
+        return sum((k == n).astype(jnp.int32) * u for n, u in enumerate(WALK))
+
+    def arrive(u):
         for q in range(2):
             split = jnp.logical_or(u == 3, u >= 12)
 
             @pl.when(jnp.logical_and(u > 0, jnp.logical_not(split)))
             def _():
                 here = nbuf.at[q, u]
-                remote(here, here, n_send.at[q, u, 0], n_recv.at[q, u, 0], mate).wait_recv()
+                remote(here, here, n_send.at[q], n_recv.at[q, u, 0], mate).wait_recv()
 
             @pl.when(split)
             def _():
                 for part in range(2):
                     here = nbuf.at[q, u, pl.ds(part * mid, mid)]
-                    remote(here, here, n_send.at[q, u, 0], n_recv.at[q, u, part], mate).wait_recv()
+                    remote(here, here, n_send.at[q], n_recv.at[q, u, part], mate).wait_recv()
 
             for cond, copy in passes(q, u):
                 @pl.when(cond)
                 def _():
                     copy().start()
 
-        @pl.when(u == 0)
+    def multiply2(t):
+        @pl.when(t == 0)
+        def _():
+            arrive(0 * t)
+            for n in range(1, LOOK):
+                arrive(walk(n + 0 * t))
+
+        pl.when(t < UNITS - LOOK)(lambda: arrive(walk(t + LOOK)))
+        u = walk(t)
+
+        @pl.when(t == 0)
         def _():
             qw_own.wait()
             qw_pair.wait()
@@ -444,11 +442,11 @@
         down_way = at4 * (u % 2) + (1 - at4) * far
         to = (z + 8 + 2 * down_way - 1) % 8
         dev = (to % 2, tok, to // 2 * 2 + c)
-        return remote(owned(q, u), zbuf.at[down_way, q, u], z_send.at[q, u], z_recv.at[down_way, q, u], dev)
+        return remote(owned(q, u), zbuf.at[down_way, q, u], z_send.at[q], z_recv.at[down_way, q, u], dev)
 
     def z_wait(q, u, side):
         here = zbuf.at[side, q, u]
-        remote(here, here, z_send.at[q, u], z_recv.at[side, q, u], mate).wait_recv()
+        remote(here, here, z_send.at[q], z_recv.at[side, q, u], mate).wait_recv()
 
     def fin_copy(q, u, local):
         one, two = offset(u % 4), offset(u // 4)
@@ -456,7 +454,7 @@
         dst = query.at[:, :, pl.ds(pl.multiple_of(y * narrow, narrow), narrow)]
         if local:
             return pltpu.make_async_copy(fin.at[u], dst, f_recv.at[y])
-        return remote(fin.at[u], dst, f_send.at[u], f_recv.at[y], (zlo, to, zhi * 2 + x % 2))
+        return remote(fin.at[u], dst, f_send, f_recv.at[y], (zlo, to, zhi * 2 + x % 2))
 
     def relay(q, u):
         r = rel(q)
@@ -500,17 +498,23 @@
                 fin_copy(q, u, False).start()
 
     def body2(t, carry):
-        @pl.when(t < UNITS)
-        def _():
-            multiply2(t)
-
+        if EARLY:
+            pl.when(t < UNITS)(lambda: multiply2(t))
         for q in range(2):
             r = rel(q)
-            u = t - LAG2 * (1 + (r - 4) * (2 * (r // 4) - 1))
-
-            @pl.when(jnp.logical_and(u >= 0, u < UNITS))
-            def _():
-                relay(q, u)
+            k = t - LAG2 * (1 + (r - 4) * (2 * (r // 4) - 1))
+
+            @pl.when(jnp.logical_and(k >= 0, k < UNITS))
+            def _():
+                relay(q, walk(k))
+
+        if not EARLY:
+            pl.when(t < UNITS)(lambda: multiply2(t))
+
+        @pl.when(jnp.logical_and(t >= OUT_AT, t < OUT_AT + 8))
+        def _():
+            for n in range(2):
+                out_start(2 * (t - OUT_AT) + n)
         return carry
 
     lax.fori_loop(0, UNITS + 5 * LAG2, body2, 0)
@@ -519,34 +523,21 @@
     for n in range(4):
         dst = query.at[:, :, pl.ds(n * narrow, narrow)]
         pltpu.make_async_copy(dst, dst, f_recv.at[n]).wait()
-    others(lambda n: stat_copy(n).wait_send())
-
-    def out_done(n, carry):
-        @pl.when(jnp.logical_not(out_self(n)))
-        def _():
-            out_copy(n, False).wait_send()
-        return carry
-
-    lax.fori_loop(0, 16, out_done, 0)
-
-    def drain2(u, carry):
-        for q in range(2):
-            for cond, copy in passes(q, u):
-                @pl.when(cond)
-                def _():
-                    copy().wait_send()
-            mate_copy(q, u).wait_send()
-
-            @pl.when(rel(q) != 0)
-            def _():
-                z_copy(q, u).wait_send()
-
-            @pl.when(jnp.logical_and(rel(q) == 0, jnp.logical_not(jnp.logical_and(u == 0, f_self))))
-            def _():
-                fin_copy(q, u, False).wait_send()
-        return carry
-
-    lax.fori_loop(0, UNITS, drain2, 0)
+    sent(stats.at[pl.ds(0, 15)], st_send)
+    for q in range(2):
+        sent(nbuf.at[q, pl.ds(0, 15)], n_send.at[q])
+        sent(cbuf.at[q], c_send.at[q])
+        pl.when(rel(q) != 0)(lambda: sent(zbuf.at[0, q], z_send.at[q]))
+    sent(rsrc.at[:, pl.ds(0, 15)], res_send.at[0])
+    res_self = zhi // 2 == zlo
+    pl.when(res_self)(lambda: sent(rbuf.at[pl.ds(0, 7)], res_send.at[1]))
+    pl.when(jnp.logical_not(res_self))(lambda: sent(rbuf, res_send.at[1]))
+    out_own = jnp.logical_and(zhi == 2 * zlo + x // 2, jnp.logical_and(c == x % 2, zlo == y // 2))
+    pl.when(out_own)(lambda: sent(rsrc.at[:, pl.ds(0, 15)], so_send))
+    pl.when(jnp.logical_not(out_own))(lambda: sent(rsrc, so_send))
+    f_dest = zhi == 2 * c + x // 2
+    pl.when(f_self)(lambda: sent(fin.at[pl.ds(0, 15)], f_send))
+    pl.when(jnp.logical_and(f_dest, jnp.logical_not(f_self)))(lambda: sent(fin, f_send))
 
 
 def per_device(
@@ -570,7 +561,8 @@
         scratch_shapes=[
             pltpu.VMEM((8, 2, rows // 2, depth), BF16),
             pltpu.VMEM((2, 16, 16, narrow), BF16),
-            pltpu.VMEM((2, 8, 16, wide), BF16),
+            pltpu.VMEM((16, 2, 16, narrow), BF16),
+            pltpu.VMEM((8, 2, 2, 16, narrow), BF16),
             pltpu.VMEM((UNITS, 4, 4, 16, width), BF16),
             pltpu.VMEM((2, UNITS, 2, 2, 16, wide), BF16),
             pltpu.VMEM((2, UNITS, 2, 4, 16, wide), BF16),
@@ -578,7 +570,7 @@
             pltpu.VMEM((2, UNITS, 2, 16, wide), BF16),
             pltpu.VMEM((UNITS, 16, wide), BF16),
             pltpu.VMEM((UNITS, 16, wide), BF16),
-            pltpu.VMEM((UNITS, 16, wide), F32),
+            pltpu.VMEM((2, 8, 16, wide), F32),
             pltpu.VMEM((2, 8, 16, wide), BF16),
             pltpu.VMEM((16, 2, 8, 128), F32),
             pltpu.VMEM((2, UNITS, 128, wide), BF16),
@@ -590,23 +582,23 @@
             dma,
             dma((24,)),
             dma((16,)),
-            dma((16,)),
-            dma,
-            dma((UNITS, 2, 5, 2)),
+            dma((2,)),
+            dma((2,)),
+            dma((2, 5)),
             dma((UNITS, 2, 5, 2)),
             dma((3,)),
             dma((2,)),
-            dma((16,)),
-            dma((16,)),
+            dma,
             dma((16,)),
             dma,
-            dma((2, UNITS, 4)),
+            dma,
+            dma((2,)),
             dma((2, UNITS, 2)),
+            dma((2,)),
             dma((2, UNITS)),
-            dma((2, UNITS)),
-            dma((2, UNITS)),
+            dma((2,)),
             dma((2, 2, UNITS)),
-            dma((UNITS,)),
+            dma,
             dma((4,)),
         ],
         compiler_params=pltpu.CompilerParams(
@@ -620,12 +612,12 @@
     )(
         hidden.reshape(2, rows // 2, depth),
         resid.reshape(2, 16, 16, narrow),
-        down_bias.reshape(1, narrow),
+        down_bias,
         down_weight,
-        norm_gain.reshape(2, 1, wide),
-        norm_shift.reshape(2, 1, wide),
+        norm_gain,
+        norm_shift,
         query_weight.reshape(2, wide, narrow),
-        jnp.broadcast_to(query_bias.reshape(4, 1, narrow), (4, 8, narrow)),
+        query_bias,
     )
     return (stream.reshape(rows, narrow), query)
 

time: 236 us -> 197 us (0.83)
  Pallas kernels: 224 us -> 190 us
  local copies, waits for them, and re-layouts: 8.72 us -> 3.55 us
    pallas_call x1, Pallas kernels: 224 us -> 190 us  [per_device(): pl.pallas_call(layer_kernel, out_shape=(jax.ShapeDtypeStruct((2, 16, 16,...]
    reshape x3 -> x0, local copies, waits for them, and re-layouts: 3.85 us -> none  [the longest x1 1.3 us: per_device(): norm_shift.reshape(2, 1, wide)]
where the time goes in v4:
time: 197 us; the launch traced here: 194 us
  Pallas kernels  190 us (96%)
  local copies, waits for them, and re-layouts  3.55 us (2%)
    pallas_call x1, Pallas kernels, per_device(): pl.pallas_call(layer_kernel, out_shape=(jax.ShapeDtypeStruct((2, 16, 16,...  190 us

profile of v4, /device:TPU:12, one launch (start us, length us, event | category | flops | bytes accessed | tf_op | source)
XLA Modules:
  0.0 194.2 jit_solution(3142244715472082236)
XLA Ops:
  0.6 190.0 %shard_map.95 = (bf16[2,16,16,384]{3,2,1,0:T(8,128)(2,1)}, bf16[8,16,1536]{2,1,0:T(8,128)(2,1)}) custom-call(bf16[2,256,768]{2,1,0:T(8,128)(2,1)} %bitcast.6, bf16[2,16,16,384]{3,2,1,0:T(8,128)(2,1)} %bitcast.7, f32[384]{0:T(512)} %bias.1, bf16[768,1536]{1,0:T(8,128)(2,1)} %weight.1, f32[1536]{0:T(1024)} %gain.1, f32[1536]{0:T(1024)} %shift.1, ...), custom_call_target="tpu_custom_call" | custom-call | flops 14495514624 | bytes 3145728 | tf_op jit(solution)/shard_map/pallas_call | solution.py:553
  190.6 1.8 copy.12
  192.4 1.8 copy.13

commit v5 on v4

--- a/solution.py
+++ b/solution.py
@@ -14,13 +14,13 @@
 UNITS = 16
 LAG = 2
 BEAT = 6
-ORDER = (0, 4, 3, 2, 1)
-PACE = True
+ORDER = (4, 3, 2, 1, 0)
 LOOK = 1
-WALK = (0, 1, 2, 4, 8, 3, 5, 9, 6, 10, 12, 7, 11, 13, 14, 15)
+WALK = (0, 1, 2, 4, 8, 5, 9, 6, 10, 3, 12, 7, 11, 13, 14, 15)
+LAG1 = 1
 LAG2 = 2
-OUT_AT = 0
-EARLY = True
+OUT_AT = -1
+EARLY = False
 
 
 def add(*terms):
@@ -71,32 +71,30 @@
     for dev in (*x_devs, *y_devs):
         greet(dev)
 
-    def greet_line(n, carry):
-        pl.when(n != me)(lambda: greet((n // 2 % 2, tok, n // 4 * 2 + n % 2)))
-        return carry
-
-    lax.fori_loop(0, 16, greet_line, 0)
+    for dev in (*z_devs, mate, pair, {"section": 1 - zlo, "wid": (zhi + 3 + 2 * zlo) % 4 * 2 + c}):
+        greet(dev)
 
     own_copy = pltpu.make_async_copy(hidden, hbuf.at[wid], own_sem)
     own_copy.start()
-    qw_own = pltpu.make_async_copy(qweight.at[zlo], qwm.at[zlo], qw_sem.at[0])
+    narrow = resid.shape[3]
+    place_at = pl.ds(pl.multiple_of((zlo + c) % 2 * narrow, narrow), narrow)
+    qw_own = pltpu.make_async_copy(qweight.at[zlo], qwm.at[:, place_at], qw_sem.at[0])
     qw_own.start()
-    narrow = resid.shape[3]
     rsrc[...] = (resid[...].astype(F32) + bias[...].reshape(1, 1, 1, -1)).astype(BF16)
     for n in range(4):
         bias2[c, n] = jnp.broadcast_to(qbias[n * narrow : (n + 1) * narrow].reshape(1, narrow), (8, narrow))
-    pl.semaphore_wait(barrier, 4 + 15)
+    pl.semaphore_wait(barrier, 4 + 5)
 
     def own_send(n):
         h = n % 2
         dev = (mate, *z_devs)[n // 2]
-        step = (2 + h, 4 + 4 * h, 5 + 4 * h)[n // 2]
+        step = (2 + h, 4 + 4 * h, 9 - 4 * h)[n // 2]
         return remote(hidden.at[h], hbuf.at[wid, h], ag_send.at[n], ag_recv.at[step], dev)
 
-    for n in (2, 4, 0, 1) if PACE else (2, 4, 0, 3, 5, 1):
+    for n in (2, 5, 0, 1):
         own_send(n).start()
 
-    qw_pair = remote(qweight.at[1 - zlo], qwm.at[zlo], qw_sem.at[1], qw_sem.at[2], pair)
+    qw_pair = remote(qweight.at[1 - zlo], qwm.at[:, place_at], qw_sem.at[1], qw_sem.at[2], pair)
     bias_mate = remote(bias2.at[c], bias2.at[c], b_sem.at[0], b_sem.at[1], mate)
     bias_mate.start()
 
@@ -104,7 +102,7 @@
         g, k = i // 4, i % 4
         mid = (g + 1) // 2 % 2
         off = mid * (3 - 2 * (k % 2)) + 2 * (g // 3)
-        h = mid * (g - 1) + (1 - mid) * (k % 2)
+        h = (k + mid * (g - 1)) % 2
         return (zhi + off) % 4 * 2 + (c + k // 2) % 2, h
 
     def mate_send(i):
@@ -178,17 +176,16 @@
         def _():
             own_copy.wait()
 
+        for step, gone, then in ((4, (2, 5), (own_send(3), own_send(4))), (8, (3, 4), (far_send(4, 0), far_send(5, 1)))):
+            @pl.when(i == step)
+            def _():
+                for n, copy in zip(gone, then):
+                    own_send(n).wait_send()
+                    copy.start()
+
         @pl.when(i >= 2)
         def _():
             remote(hbuf.at[w, h], hbuf.at[w, h], ag_send.at[0], ag_recv.at[i], mate).wait_recv()
-
-        copies = ((8, far_send(4, 0)), (9, far_send(9, 1)))
-        if PACE:
-            copies = ((4, own_send(3)), (5, own_send(5)), *copies)
-        else:
-            copies = ((4, far_send(4, 0)), (9, far_send(9, 1)))
-        for step, copy in copies:
-            pl.when(i == step)(copy.start)
 
         @pl.when(jnp.logical_and(i >= 4, i % 4 < 2))
         def _():
@@ -320,17 +317,24 @@
         pl.when(out_self(n))(lambda: out_copy(n, True).start())
         pl.when(jnp.logical_not(out_self(n)))(lambda: out_copy(n, False).start())
 
-    for n in range(6):
+    for n in range(2):
         own_send(n).wait_send()
     for i in (4, 5, 8, 9, 12, 13):
         mate_send(i).wait_send()
     far_send(4, 0).wait_send()
-    far_send(9, 1).wait_send()
+    far_send(5, 1).wait_send()
 
     for a in range(2):
         for n, ref in enumerate((r1, r2, r3, r4)):
             sent(ref.at[a], rs_send.at[a, n])
     sent(zr, rs_send.at[0, 4])
+
+    if OUT_AT < 0:
+        def out_each(n, carry):
+            out_start(n)
+            return carry
+
+        lax.fori_loop(0, 16, out_each, 0)
 
     def stat_wait(n):
         here = stats.at[n]
@@ -348,16 +352,16 @@
         both = jnp.where(row == 0, mean, scale).T
         values = sbuf[q].reshape(tokens, wide).astype(F32)
         normed = (values - both[:, 0:1]) * both[:, 1:2] * gains + shifts
-        nbuf[q, 0] = normed.astype(BF16)
+        nbuf[0, q] = normed.astype(BF16)
 
     mid = tokens // 2
 
     def pass_on(q, u, to, dev, part=None):
         if part is None:
-            src, dst = nbuf.at[q, u], nbuf.at[q, to]
+            src, dst = nbuf.at[u, q], nbuf.at[to, q]
         else:
             rows = pl.ds(part * mid, mid)
-            src, dst = nbuf.at[q, u, rows], nbuf.at[q, to, rows]
+            src, dst = nbuf.at[u, q, rows], nbuf.at[to, q, rows]
         return remote(src, dst, n_send.at[q], n_recv.at[q, to, part or 0], dev)
 
     def passes(q, u):
@@ -394,13 +398,13 @@
 
             @pl.when(jnp.logical_and(u > 0, jnp.logical_not(split)))
             def _():
-                here = nbuf.at[q, u]
+                here = nbuf.at[u, q]
                 remote(here, here, n_send.at[q], n_recv.at[q, u, 0], mate).wait_recv()
 
             @pl.when(split)
             def _():
                 for part in range(2):
-                    here = nbuf.at[q, u, pl.ds(part * mid, mid)]
+                    here = nbuf.at[u, q, pl.ds(part * mid, mid)]
                     remote(here, here, n_send.at[q], n_recv.at[q, u, part], mate).wait_recv()
 
             for cond, copy in passes(q, u):
@@ -415,7 +419,6 @@
             for n in range(1, LOOK):
                 arrive(walk(n + 0 * t))
 
-        pl.when(t < UNITS - LOOK)(lambda: arrive(walk(t + LOOK)))
         u = walk(t)
 
         @pl.when(t == 0)
@@ -424,13 +427,12 @@
             qw_pair.wait()
             bias_mate.wait()
 
+        rows = nbuf[u].reshape(2 * tokens, wide)
+        part = jnp.dot(rows, qwm[...], preferred_element_type=F32)
+        pbuf[u, :, :, :, pl.ds(0, 2 * narrow)] = part.astype(BF16).reshape(4, 4, 16, 2 * narrow)
         for q in range(2):
-            rows = nbuf[q, u]
-            part = jnp.dot(rows, qwm[1 - c], preferred_element_type=F32)
-            given(q, u)[...] = part.astype(BF16).reshape(2, 4, 16, narrow)
             mate_copy(q, u).start()
-            part = jnp.dot(rows, qwm[c], preferred_element_type=F32)
-            owned(q, u)[...] = part.astype(BF16).reshape(2, 4, 16, narrow)
+        pl.when(t < UNITS - LOOK)(lambda: arrive(walk(t + LOOK)))
 
     def rel(q):
         return (z + 16 - 2 * (2 * c + x // 2) - q) % 8
@@ -502,7 +504,7 @@
             pl.when(t < UNITS)(lambda: multiply2(t))
         for q in range(2):
             r = rel(q)
-            k = t - LAG2 * (1 + (r - 4) * (2 * (r // 4) - 1))
+            k = t - LAG1 - LAG2 * ((r - 4) * (2 * (r // 4) - 1))
 
             @pl.when(jnp.logical_and(k >= 0, k < UNITS))
             def _():
@@ -511,13 +513,13 @@
         if not EARLY:
             pl.when(t < UNITS)(lambda: multiply2(t))
 
-        @pl.when(jnp.logical_and(t >= OUT_AT, t < OUT_AT + 8))
+        @pl.when(jnp.logical_and(t >= OUT_AT, t < OUT_AT + (8 if OUT_AT >= 0 else 0)))
         def _():
             for n in range(2):
                 out_start(2 * (t - OUT_AT) + n)
         return carry
 
-    lax.fori_loop(0, UNITS + 5 * LAG2, body2, 0)
+    lax.fori_loop(0, UNITS + LAG1 + 4 * LAG2, body2, 0)
 
     pltpu.make_async_copy(stream, stream, so_recv).wait()
     for n in range(4):
@@ -525,7 +527,7 @@
         pltpu.make_async_copy(dst, dst, f_recv.at[n]).wait()
     sent(stats.at[pl.ds(0, 15)], st_send)
     for q in range(2):
-        sent(nbuf.at[q, pl.ds(0, 15)], n_send.at[q])
+        sent(nbuf.at[pl.ds(0, 15), q], n_send.at[q])
         sent(cbuf.at[q], c_send.at[q])
         pl.when(rel(q) != 0)(lambda: sent(zbuf.at[0, q], z_send.at[q]))
     sent(rsrc.at[:, pl.ds(0, 15)], res_send.at[0])
@@ -573,8 +575,8 @@
             pltpu.VMEM((2, 8, 16, wide), F32),
             pltpu.VMEM((2, 8, 16, wide), BF16),
             pltpu.VMEM((16, 2, 8, 128), F32),
-            pltpu.VMEM((2, UNITS, 128, wide), BF16),
-            pltpu.VMEM((2, wide, narrow), BF16),
+            pltpu.VMEM((UNITS, 2, 128, wide), BF16),
+            pltpu.VMEM((wide, 2 * narrow), BF16),
             pltpu.VMEM((2, 4, 8, narrow), F32),
             pltpu.VMEM((2, UNITS, 2, 4, 16, narrow), BF16),
             pltpu.VMEM((2, 2, UNITS, 2, 4, 16, narrow), BF16),

time: 197 us -> 187 us (0.949); the launches traced: 194 us -> 186 us
  Pallas kernels: 190 us -> 182 us
    pallas_call x1, Pallas kernels: 190 us -> 182 us  [per_device(): pl.pallas_call(layer_kernel, out_shape=(jax.ShapeDtypeStruct((2, 16, 16,...]
where the time goes in v5:
time: 187 us; the launch traced here: 186 us
  Pallas kernels  182 us (97%)
  local copies, waits for them, and re-layouts  3.55 us (2%)
    pallas_call x1, Pallas kernels, per_device(): pl.pallas_call(layer_kernel, out_shape=(jax.ShapeDtypeStruct((2, 16, 16,...  182 us

profile of v5, /device:TPU:12, one launch (start us, length us, event | category | flops | bytes accessed | tf_op | source)
XLA Modules:
  0.0 186.5 jit_solution(10325192785383428650)
XLA Ops:
  0.6 182.3 %shard_map.95 = (bf16[2,16,16,384]{3,2,1,0:T(8,128)(2,1)}, bf16[8,16,1536]{2,1,0:T(8,128)(2,1)}) custom-call(bf16[2,256,768]{2,1,0:T(8,128)(2,1)} %bitcast.6, bf16[2,16,16,384]{3,2,1,0:T(8,128)(2,1)} %bitcast.7, f32[384]{0:T(512)} %bias.1, bf16[768,1536]{1,0:T(8,128)(2,1)} %weight.1, f32[1536]{0:T(1024)} %gain.1, f32[1536]{0:T(1024)} %shift.1, ...), custom_call_target="tpu_custom_call" | custom-call | flops 14495514624 | bytes 3145728 | tf_op jit(solution)/shard_map/pallas_call | solution.py:555
  182.9 1.8 copy.12
  184.7 1.8 copy.13

commit v6 on v5

--- a/solution.py
+++ b/solution.py
@@ -191,8 +191,8 @@
         def _():
             mate_send(i).start()
 
-        pl.when(i == 12)(res_turn)
-        pl.when(i == 13)(qw_pair.start)
+        pl.when(i == 10)(res_turn)
+        pl.when(i == 8)(qw_pair.start)
 
         rows = hbuf[w, h]
         for n in range(0, 2 * wide, 512):
@@ -264,6 +264,13 @@
         def _():
             for n in range(4):
                 res_start(4 * (t - 4 * LAG - 1) + n)
+
+        end = 3 * BEAT + 4 * LAG
+
+        @pl.when(t >= end)
+        def _():
+            for n in range(3):
+                finish(3 * (t - end) + n)
         return carry
 
     lax.fori_loop(0, 3 * BEAT + 4 + 4 * LAG, body, 0)
@@ -272,7 +279,7 @@
         finish(i)
         return carry
 
-    lax.fori_loop(0, UNITS, finish_each, 0)
+    lax.fori_loop(12, UNITS, finish_each, 0)
 
     sent(rbuf, res_recv.at[1])
     for q in range(2):

time: 187 us -> 186 us (level)
  no operation moved by 1% of the time
where the time goes in v6:
time: 186 us
  Pallas kernels  181 us (97%)
  local copies, waits for them, and re-layouts  3.55 us (2%)
    pallas_call x1, Pallas kernels, per_device(): pl.pallas_call(layer_kernel, out_shape=(jax.ShapeDtypeStruct((2, 16, 16,...  181 us

profile of v6, /device:TPU:12, one launch (start us, length us, event | category | flops | bytes accessed | tf_op | source)
XLA Modules:
  0.0 185.5 jit_solution(16041926506388963625)
XLA Ops:
  0.6 181.3 %shard_map.95 = (bf16[2,16,16,384]{3,2,1,0:T(8,128)(2,1)}, bf16[8,16,1536]{2,1,0:T(8,128)(2,1)}) custom-call(bf16[2,256,768]{2,1,0:T(8,128)(2,1)} %bitcast.6, bf16[2,16,16,384]{3,2,1,0:T(8,128)(2,1)} %bitcast.7, f32[384]{0:T(512)} %bias.1, bf16[768,1536]{1,0:T(8,128)(2,1)} %weight.1, f32[1536]{0:T(1024)} %gain.1, f32[1536]{0:T(1024)} %shift.1, ...), custom_call_target="tpu_custom_call" | custom-call | flops 14495514624 | bytes 3145728 | tf_op jit(solution)/shard_map/pallas_call | solution.py:562
  182.0 1.8 copy.12
  183.8 1.8 copy.13
